TPU v7x, 32 devices: a whole 2x2x4 slice. The times are simulated.
32 devices in a mesh: gx: 2 (over core), gy: 4 (over y, x), gz: 4 (over z).
Axes of the slice: x: 2, y: 2, z: 4, core: 2. Of those that a mesh axis runs over, the one named last changes fastest.
Arguments:
- species_field: float32 [48, 2048, 2048], P('gz', 'gx', 'gy')
- x_mode_basis: float32 [2048, 256], P('gx'), may hold values from -0.125 to 0.125
- y_mode_basis: float32 [2048, 256], P('gy'), may hold values from -0.125 to 0.125
Outputs:
- gram_x: float32 [2048, 2048], P(('gx', 'gy'))
- gram_y: float32 [2048, 2048], P('gy', 'gx')
- reduced_core_tensor: float32 [256, 48, 256], P('gx', 'gz', 'gy')
All inputs are finite; a program needn't handle non-finite values.
Results may differ from a plain program's by a relative error of at most 0.000092.
Values sent between devices are 32-bit elements; how exact they have to be, the bound alone decides.
A program may use at most 128 MiB of HBM per device.

v0:
```python
import jax
import jax.numpy as jnp
from jax import lax
from jax.sharding import PartitionSpec as P


def per_device(species_field, x_mode_basis, y_mode_basis):
    exact_precision = lax.Precision.HIGHEST
    total_y = species_field.shape[2] * lax.axis_size("gy")
    total_slices = species_field.shape[0] * lax.axis_size("gz")
    fibers = lax.all_to_all(species_field, "gx", split_axis=0, concat_axis=1, tiled=True)
    partial_value = jnp.einsum("sxy,szy->xz", fibers, fibers, precision=exact_precision)
    rows_x = lax.psum_scatter(partial_value, ("gx", "gy"), scatter_dimension=0, tiled=True)
    rows_x = rows_x / (total_y * total_slices)
    gram_x = lax.psum(rows_x, "gz")
    reduced_result = lax.psum_scatter(
        jnp.einsum("xr,sxy->rsy", x_mode_basis, species_field, precision=exact_precision),
        "gx",
        scatter_dimension=0,
        tiled=True,
    )
    columns = jnp.einsum(
        "rsy,rsz->yz",
        reduced_result,
        lax.all_gather(reduced_result, "gy", axis=2, tiled=True),
        precision=exact_precision,
    )
    rank_total = x_mode_basis.shape[1]
    part_y = lax.psum_scatter(columns, "gx", scatter_dimension=1, tiled=True) / (
        rank_total * total_slices
    )
    core_term_list = jnp.einsum(
        "mtl,lw->mtw", reduced_result, y_mode_basis, precision=exact_precision
    )
    reduced_core_tensor = lax.psum_scatter(core_term_list, "gy", scatter_dimension=2, tiled=True)
    gram_y = lax.psum(part_y, "gz")
    return (gram_x, gram_y, reduced_core_tensor)


def solution(mesh):
    in_specs = (P("gz", "gx", "gy"), P("gx", None), P("gy", None))
    out_specs = (P(("gx", "gy"), None), P("gy", "gx"), P("gx", "gz", "gy"))
    return jax.shard_map(
        per_device, mesh=mesh, in_specs=in_specs, out_specs=out_specs, check_vma=False
    )
```

profile of v0, /device:TPU:0, one launch (start us, length us, event | category | flops | bytes accessed | tf_op | source)
XLA Modules:
  0.0 559.4 jit_solution(12859257955429422321)
XLA Ops:
  8.0 0.0 copy-start
  8.0 0.0 reduce-scatter.7.cloned.1.call-start
  8.1 1.2 copy-done
  9.2 25.8 %fusion = f32[256,12,512]{2,0,1:T(8,128)} fusion(f32[12,1024,512]{2,1,0:T(8,128)} %param.3, f32[1024,256]{1,0:T(8,128)S(1)} %copy-done), kind=kOutput, calls=%fused_computation.2 | convolution fusion | flops 19327352832 | bytes 32505856 | tf_op jit(solution)/shard_map/xr,sxy->rsy/dot_general | solution.py:17
  35.1 0.0 reduce-scatter.7.cloned.1.call-update
  35.1 0.0 all-gather.2.cloned.1.call-start
  35.1 17.3 %reduce-scatter.7.cloned.1.call-done = f32[128,12,512]{2,0,1:T(8,128)} async-done(((f32[256,12,512]{2,0,1:T(8,128)}), f32[128,12,512]{2,0,1:T(8,128)}) %reduce-scatter.7.cloned.1.call-update) | async-done | bytes 3145744 | tf_op jit(solution)/shard_map/reduce_scatter | solution.py:16
  52.4 0.0 all-gather.2.cloned.1.call-update
  52.5 0.0 reduce-scatter.5.cloned.1.call-start
  52.5 26.5 %all_to_all.18 = f32[12,1024,512]{2,1,0:T(8,128)S(1)} all-to-all(f32[12,1024,512]{2,1,0:T(8,128)} %param.3), channel_id=1, replica_groups=mesh['gx'=2,'gy'=4,'gz'=4] {'gx'}, dimensions={0} | all-to-all | bytes 50331648 | tf_op jit(solution)/shard_map/all_to_all | solution.py:11
  79.0 8.7 %copy.6 = f32[2,6,1024,512]{3,2,0,1:T(8,128)} copy(f32[2,6,1024,512]{3,2,1,0:T(8,128)S(1)} %bitcast.20) | data formatting | bytes 50331648 | tf_op jit(solution)/shard_map/all_to_all | solution.py:11
  87.7 168.2 %convolution_bitcast_fusion = f32[2048,2048]{1,0:T(8,128)} fusion(f32[6,2048,512]{2,1,0:T(8,128)} %bitcast.21), kind=kOutput, calls=%fused_computation | convolution fusion | flops 154618822656 | bytes 41943040 | tf_op jit(solution)/shard_map/sxy,szy->xz/dot_general | solution.py:12
  255.9 0.0 reduce-scatter.5.cloned.1.call-update
  256.0 0.3 reduce-scatter.9.cloned.1.call-start
  256.2 0.0 all-gather.2.cloned.1.call-done
  256.3 24.5 %convolution_bitcast_fusion.1 = f32[512,2048]{1,0:T(8,128)} fusion(f32[128,12,512]{2,0,1:T(8,128)} %reduce-scatter.7.cloned.1.call-done, f32[128,12,2048]{2,0,1:T(8,128)} %all-gather.2.cloned.1.call-done), kind=kOutput, calls=%fused_computation.1 | convolution fusion | flops 19327352832 | bytes 19922944 | tf_op jit(solution)/shard_map/rsy,rsz->yz/dot_general | solution.py:22
  280.8 0.0 copy-start.3
  280.8 0.0 reduce-scatter.9.cloned.1.call-update
  280.8 0.0 reduce-scatter.11.cloned.1.call-start
  280.9 1.0 copy-done.3
  281.9 5.7 %fusion.2 = f32[128,12,256]{0,2,1:T(8,128)} fusion(f32[128,12,512]{2,0,1:T(8,128)} %reduce-scatter.7.cloned.1.call-done, f32[512,256]{1,0:T(8,128)S(1)} %copy-done.3), kind=kOutput, calls=%fused_computation.6 | convolution fusion | flops 2415919104 | bytes 5242880 | tf_op jit(solution)/shard_map/mtl,lw->mtw/dot_general | solution.py:32
  287.6 0.0 reduce-scatter.11.cloned.1.call-update
  287.7 0.0 all-reduce.3.cloned.1.call-start
  287.7 85.4 %reduce-scatter.5.cloned.1.call-done = f32[256,2048]{1,0:T(8,128)} async-done(((f32[2048,2048]{1,0:T(8,128)}), f32[256,2048]{1,0:T(8,128)}) %reduce-scatter.5.cloned.1.call-update) | async-done | bytes 2097168 | tf_op jit(solution)/shard_map/reduce_scatter | solution.py:13
  373.1 3.2 broadcast_multiply_fusion.1
  376.3 11.1 %reduce-scatter.9.cloned.1.call-done = f32[512,1024]{1,0:T(8,128)} async-done(((f32[512,2048]{1,0:T(8,128)}), f32[512,1024]{1,0:T(8,128)}) %reduce-scatter.9.cloned.1.call-update) | async-done | bytes 2097168 | tf_op jit(solution)/shard_map/reduce_scatter | solution.py:29
  387.3 3.3 broadcast_multiply_fusion
  390.6 0.0 all-reduce.3.cloned.1.call-update
  390.7 32.6 %reduce-scatter.11.cloned.1.call-done = f32[128,12,64]{0,2,1:T(8,128)} async-done(((f32[128,12,256]{0,2,1:T(8,128)}), f32[128,12,64]{0,2,1:T(8,128)}) %reduce-scatter.11.cloned.1.call-update) | async-done | bytes 393232 | tf_op jit(solution)/shard_map/reduce_scatter | solution.py:35
  423.2 124.2 %all-reduce.3.cloned.1.call-done = (f32[256,2048]{1,0:T(8,128)}, f32[512,1024]{1,0:T(8,128)}) async-done(((f32[256,2048]{1,0:T(8,128)}, f32[512,1024]{1,0:T(8,128)}), (f32[256,2048]{1,0:T(8,128)}, f32[512,1024]{1,0:T(8,128)})) %all-reduce.3.cloned.1.call-update) | async-done | bytes 4194320 | tf_op jit(solution)/shard_map/psum | solution.py:15
  547.4 0.0 copy-start.2
  547.4 0.0 copy-start.1
  547.4 3.3 copy.17
  550.7 0.0 copy-done.2
  550.7 1.3 copy.18
  552.1 0.0 copy-done.1
Async XLA Ops:
  8.0 1.2 copy-start
  8.0 44.4 %reduce-scatter.7.cloned.1.call-start = ((), (), s32[]{:S(2)}) async-start(), calls=%async_computation.6 | async-start | bytes 9437184 | tf_op jit(solution)/shard_map/reduce_scatter | solution.py:16
  35.1 221.2 %all-gather.2.cloned.1.call-start = ((), (), s32[]{:S(2)}) async-start(), calls=%async_computation.7 | async-start | bytes 15728640 | tf_op jit(solution)/shard_map/all_gather | solution.py:25
  52.5 320.6 %reduce-scatter.5.cloned.1.call-start = ((), (), s32[]{:S(2)}) async-start(), calls=%async_computation.5 | async-start | bytes 18874368 | tf_op jit(solution)/shard_map/reduce_scatter | solution.py:13
  256.0 131.4 %reduce-scatter.9.cloned.1.call-start = ((), (), s32[]{:S(2)}) async-start(), calls=%async_computation.8 | async-start | bytes 6291456 | tf_op jit(solution)/shard_map/reduce_scatter | solution.py:29
  280.8 1.1 copy-start.3
  280.8 142.4 %reduce-scatter.11.cloned.1.call-start = ((), (), s32[]{:S(2)}) async-start(), calls=%async_computation.9 | async-start | bytes 1966080 | tf_op jit(solution)/shard_map/reduce_scatter | solution.py:35
  287.7 259.8 %all-reduce.3.cloned.1.call-start = ((), (), s32[]{:S(2)}) async-start(), calls=%async_computation.10 | async-start | bytes 8388608 | tf_op jit(solution)/shard_map/psum | solution.py:15
  547.4 3.3 copy-start.2
  547.4 4.6 copy-start.1
Sparse Core Ops, SparseCore 0:
  35.2 17.1 reduce-scatter.6
  54.4 123.6 all-gather.1
  390.8 156.6 all-reduce.2
Sparse Core Ops, SparseCore 1:
  256.0 117.0 reduce-scatter.4
  375.3 12.0 reduce-scatter.8
  391.0 32.1 reduce-scatter.10
where the time goes:
time: 560 us; the launch traced here: 559 us
  waiting for transfers between devices  271 us (48%)
  matrix products  224 us (40%)
  blocking collectives  26.5 us (5%)
  local copies, waits for them, and re-layouts  15.5 us (3%)
  between operations  15.5 us (3%)
  other arithmetic  6.5 us (1%)
    dot_general x1, matrix products, per_device(): jnp.einsum('sxy,szy->xz', fibers, fibers, precision=exact_precision)  168 us
    psum x1, waiting for transfers between devices, per_device(): gram_x = lax.psum(rows_x, 'gz')  124 us
    reduce_scatter x1, waiting for transfers between devices, per_device(): lax.psum_scatter(partial_value, ('gx', 'gy'), scatter_dimension=0, tiled=...  85.4 us
    reduce_scatter x1, waiting for transfers between devices, per_device(): lax.psum_scatter(core_term_list, 'gy', scatter_dimension=2, tiled=True)  32.6 us
    all_to_all x1, blocking collectives, per_device(): lax.all_to_all(species_field, 'gx', split_axis=0, concat_axis=1, tiled=True)  26.5 us
    dot_general x1, matrix products, per_device(): jnp.einsum('xr,sxy->rsy', x_mode_basis, species_field, precision=exact_pr...  25.8 us
    dot_general x1, matrix products, per_device(): jnp.einsum('rsy,rsz->yz', reduced_result, lax.all_gather(reduced_result,...  24.5 us
    reduce_scatter x1, waiting for transfers between devices, per_device(): lax.psum_scatter(jnp.einsum('xr,sxy->rsy', x_mode_basis, species_field, p...  17.3 us
  transfers between devices with their start and end apart: 6, of which 5 were waited for; matrix products, arithmetic and copies ran while one was open for 38% of the time, Pallas kernels for 0%

commit v1 on v0

v1 whole, which is shorter than its diff:
```python
import functools

import jax
import jax.numpy as jnp
from jax import lax
from jax.experimental import pallas as pl
from jax.experimental.pallas import tpu as pltpu
from jax.sharding import PartitionSpec as P

F32, BF16 = jnp.float32, jnp.bfloat16
LIMIT = 50 * 2**20


def split(x):
    hi = x.astype(BF16)
    return hi, (x - hi.astype(F32)).astype(BF16)


def dot(a, b, dims):
    return lax.dot_general(a, b, (dims, ((), ())), preferred_element_type=F32)


def project_kernel(u_ref, x_ref, keep_ref, send_ref):
    u_hi, u_lo = split(u_ref[...])
    x_hi, x_lo = split(x_ref[0])
    out = dot(
        jnp.concatenate([u_hi, u_hi, u_lo], axis=1),
        jnp.concatenate([x_hi, x_lo, x_hi], axis=0),
        ((1,), (0,)),
    )
    half = keep_ref.shape[1]
    keep_ref[0] = out[:half]
    send_ref[0] = out[half:]


def project(field, basis):
    slices, rows, cols = field.shape
    rank = basis.shape[0]
    out = jax.ShapeDtypeStruct((slices, rank // 2, cols), F32)
    block = pl.BlockSpec((1, rank // 2, cols), lambda s: (s, 0, 0))
    return pl.pallas_call(
        project_kernel,
        grid=(slices,),
        in_specs=[
            pl.BlockSpec((rank, rows), lambda s: (0, 0)),
            pl.BlockSpec((1, rows, cols), lambda s: (s, 0, 0)),
        ],
        out_specs=[block, block],
        out_shape=[out, out],
        compiler_params=pltpu.CompilerParams(vmem_limit_bytes=LIMIT),
        cost_estimate=pl.CostEstimate(
            flops=6 * slices * rows * cols * rank,
            bytes_accessed=4 * slices * cols * (rows + rank),
            transcendentals=0,
        ),
    )(basis, field)


def same_half_kernel(parts, x_ref, out_ref, a_ref, b_ref):
    rows, cols = x_ref.shape[1:]
    b = rows // parts
    wide = out_ref.shape[2]

    @pl.when(pl.program_id(0) == 0)
    def _():
        out_ref[...] = jnp.zeros_like(out_ref)

    hi, lo = split(x_ref[0])
    for n, v in enumerate((hi, hi, lo)):
        a_ref[:, n * cols : (n + 1) * cols] = v
    for n, v in enumerate((hi, lo, hi)):
        b_ref[:rows, n * cols : (n + 1) * cols] = v
        b_ref[rows:, n * cols : (n + 1) * cols] = v[: b_ref.shape[0] - rows]
    for i in range(parts):
        out_ref[i] += dot(a_ref[i * b : (i + 1) * b], b_ref[i * b : i * b + wide], ((1,), (1,)))


def same_half(field, parts):
    slices, rows, cols = field.shape
    b = rows // parts
    wide = b * (parts // 2 + 1)
    return pl.pallas_call(
        functools.partial(same_half_kernel, parts),
        grid=(slices,),
        in_specs=[pl.BlockSpec((1, rows, cols), lambda s: (s, 0, 0))],
        out_specs=pl.BlockSpec((parts, b, wide), lambda s: (0, 0, 0)),
        out_shape=jax.ShapeDtypeStruct((parts, b, wide), F32),
        scratch_shapes=[
            pltpu.VMEM((rows, 3 * cols), BF16),
            pltpu.VMEM((rows + wide - b, 3 * cols), BF16),
        ],
        compiler_params=pltpu.CompilerParams(vmem_limit_bytes=LIMIT),
        cost_estimate=pl.CostEstimate(
            flops=6 * slices * rows * cols * wide,
            bytes_accessed=4 * slices * cols * rows,
            transcendentals=0,
        ),
    )(field)


def cross_kernel(gx_ref, own_ref, other_ref, out_ref, a_ref, b_ref):
    rows, cols = own_ref.shape[1:]

    @pl.when(pl.program_id(0) == 0)
    def _():
        out_ref[...] = jnp.zeros_like(out_ref)

    first = gx_ref[0] == 0
    own, other = own_ref[0], other_ref[0]
    hi, lo = split(jnp.where(first, own, other))
    for n, v in enumerate((hi, hi, lo)):
        a_ref[:, n * cols : (n + 1) * cols] = v
    hi, lo = split(jnp.where(first, other, own))
    for n, v in enumerate((hi, lo, hi)):
        b_ref[:, n * cols : (n + 1) * cols] = v
    b = min(rows, 256)
    for i in range(0, rows, b):
        out_ref[i : i + b] += dot(a_ref[i : i + b], b_ref[...], ((1,), (1,)))


def cross(gx, field, other):
    slices, rows, cols = other.shape
    return pl.pallas_call(
        cross_kernel,
        grid_spec=pltpu.PrefetchScalarGridSpec(
            num_scalar_prefetch=1,
            grid=(slices,),
            in_specs=[
                pl.BlockSpec((1, rows, cols), lambda s, g: (g[0] * slices + s, 0, 0)),
                pl.BlockSpec((1, rows, cols), lambda s, g: (s, 0, 0)),
            ],
            out_specs=pl.BlockSpec((rows, rows), lambda s, g: (0, 0)),
            scratch_shapes=[pltpu.VMEM((rows, 3 * cols), BF16)] * 2,
        ),
        out_shape=jax.ShapeDtypeStruct((rows, rows), F32),
        compiler_params=pltpu.CompilerParams(vmem_limit_bytes=LIMIT),
        cost_estimate=pl.CostEstimate(
            flops=6 * slices * rows * cols * rows,
            bytes_accessed=8 * slices * cols * rows,
            transcendentals=0,
        ),
    )(jnp.reshape(gx, (1,)).astype(jnp.int32), field, other)


def gram_y_kernel(y_ref, out_ref, b_ref):
    parts, depth, cols = y_ref.shape
    wide = out_ref.shape[2]
    i = pl.program_id(0)

    @pl.when(i == 0)
    def _():
        for j in range(b_ref.shape[1] // cols):
            hi, lo = split(y_ref[j % parts])
            b_ref[:, j * cols : (j + 1) * cols] = jnp.concatenate([hi, lo, hi], axis=0)

    hi, lo = split(jnp.transpose(y_ref[i]))
    a = jnp.concatenate([hi, hi, lo], axis=1)
    start = pl.multiple_of(i * cols, cols)
    out_ref[0] = dot(a, b_ref[:, pl.ds(start, wide)], ((1,), (0,)))


def gram_y_terms(y):
    parts, depth, cols = y.shape
    wide = cols * (parts // 2 + 1)
    return pl.pallas_call(
        gram_y_kernel,
        grid=(parts,),
        in_specs=[pl.BlockSpec((parts, depth, cols), lambda i: (0, 0, 0))],
        out_specs=pl.BlockSpec((1, cols, wide), lambda i: (i, 0, 0)),
        out_shape=jax.ShapeDtypeStruct((parts, cols, wide), F32),
        scratch_shapes=[pltpu.VMEM((3 * depth, parts * cols + wide - cols), BF16)],
        compiler_params=pltpu.CompilerParams(vmem_limit_bytes=LIMIT),
        cost_estimate=pl.CostEstimate(
            flops=6 * parts * depth * cols * wide,
            bytes_accessed=4 * parts * cols * (wide + depth),
            transcendentals=0,
        ),
    )(y)


def swap(x, axis_name):
    return lax.ppermute(x, axis_name, [(0, 1), (1, 0)])


def unroll(piece, gy, parts):
    b = piece.shape[1] // (parts // 2 + 1)
    blocks = [piece[:, k * b : (k + 1) * b] for k in range(parts // 2 + 1)]
    mirrored = []
    for k in range(parts // 2 + 1, parts):
        step = parts - k
        perm = [(i, (i + step) % parts) for i in range(parts)]
        mirrored.append(lax.ppermute(blocks[step], "gy", perm).T)
    full = jnp.concatenate(blocks + mirrored, axis=1)
    twice = jnp.concatenate([full, full], axis=1)
    return lax.dynamic_slice_in_dim(twice, ((parts - gy) % parts) * b, parts * b, axis=1)


def per_device(field, x_basis, y_basis):
    gx, gy = lax.axis_index("gx"), lax.axis_index("gy")
    parts, planes = lax.axis_size("gy"), lax.axis_size("gz")
    slices, rows, cols = field.shape
    rank = x_basis.shape[1]
    total_y, total_slices = cols * parts, slices * planes
    half = slices // 2

    basis = jnp.roll(x_basis.T, -gx * (rank // 2), axis=0)
    keep, send = project(field, basis)
    reduced = keep + swap(send, "gx")

    other = swap(lax.dynamic_slice_in_dim(field, (1 - gx) * half, half, axis=0), "gx")

    share = slices * (rank // 2) // parts
    y_rows = lax.all_to_all(reduced.reshape(parts, share, cols), "gy", 0, 0, tiled=True)
    y_basis_all = lax.all_gather(y_basis, "gy", axis=0)

    same = same_half(field, parts)
    across = cross(gx, field, other)

    b = rows // parts
    across = across.reshape(parts, b, 2, rows // 2)
    mine = lax.dynamic_index_in_dim(across, gx, axis=2, keepdims=False)
    theirs = swap(lax.dynamic_index_in_dim(across, 1 - gx, axis=2, keepdims=False), "gx")
    packed = jnp.concatenate([same, mine + theirs], axis=2)
    packed = lax.psum_scatter(packed, "gy", scatter_dimension=0, tiled=True)[0]
    packed = lax.psum(packed, "gz") / (total_y * total_slices)

    terms = gram_y_terms(y_rows)
    wide = terms.shape[2]
    terms = terms.reshape(parts, 2, cols // 2, wide)
    mine = lax.dynamic_index_in_dim(terms, gx, axis=1, keepdims=False)
    theirs = swap(lax.dynamic_index_in_dim(terms, 1 - gx, axis=1, keepdims=False), "gx")
    part_y = lax.psum_scatter(mine + theirs, "gy", scatter_dimension=0, tiled=True)[0]
    part_y = lax.psum(part_y, "gz") / (rank * total_slices)

    core = jnp.einsum("gkl,glq->kq", y_rows, y_basis_all, precision=lax.Precision.HIGH)
    q = core.shape[1]
    core = lax.all_to_all(
        core.reshape(share, parts, q // parts).transpose(1, 0, 2), "gy", 0, 0, tiled=True
    )
    core = core.reshape(slices, rank // 2, q // parts).transpose(1, 0, 2)

    wide_x = same.shape[2]
    diagonal = unroll(packed[:, :wide_x], gy, parts)
    mine = packed[:, wide_x:]
    theirs = swap(mine, "gx")
    strip = jnp.where(
        gx == 0,
        jnp.concatenate([mine, theirs], axis=1),
        jnp.concatenate([theirs, mine], axis=1),
    )
    columns = lax.all_to_all(
        strip.reshape(b, parts, b).transpose(1, 2, 0), "gy", 0, 0, tiled=True
    )
    columns = columns.transpose(1, 0, 2).reshape(b, rows)
    gram_x = jnp.where(
        gx == 0,
        jnp.concatenate([diagonal, strip], axis=1),
        jnp.concatenate([columns, diagonal], axis=1),
    )

    theirs = swap(part_y, "gx")
    both = jnp.where(
        gx == 0,
        jnp.concatenate([part_y, theirs], axis=0),
        jnp.concatenate([theirs, part_y], axis=0),
    )
    both = unroll(both, gy, parts)
    gram_y = lax.dynamic_slice_in_dim(both, gx * (total_y // 2), total_y // 2, axis=1)
    return (gram_x, gram_y, core)


def solution(mesh):
    in_specs = (P("gz", "gx", "gy"), P("gx", None), P("gy", None))
    out_specs = (P(("gx", "gy"), None), P("gy", "gx"), P("gx", "gz", "gy"))
    return jax.shard_map(
        per_device, mesh=mesh, in_specs=in_specs, out_specs=out_specs, check_vma=False
    )
```

time: 560 us -> 518 us (0.925)
  matrix products: 224 us -> 4.19 us
  Pallas kernels: 0 us -> 89.9 us
  local copies, waits for them, and re-layouts: 15.5 us -> 69.9 us
  other arithmetic: 6.5 us -> 35.7 us
  blocking collectives: 26.5 us -> 0 us
  starting transfers between devices: 0.47 us -> 18.5 us
  waiting for transfers between devices: 271 us -> 284 us
    dot_general x4 -> x1, matrix products: 224 us -> 4.19 us  [per_device(): jnp.einsum('gkl,glq->kq', y_rows, y_basis_all, precision=lax.Precision.HIGH)]
    reduce_scatter x4 -> x0, waiting for transfers between devices: 146 us -> none  [the longest x1 85.4 us: per_device(): lax.psum_scatter(partial_value, ('gx', 'gy'), scatter_dimension=0, tiled=...]
    pallas_call x0 -> x4, Pallas kernels: none -> 89.9 us  [the longest x1 33.9 us: same_half(): pl.pallas_call(functools.partial(same_half_kernel, parts), grid=(slices,)...]
    unnamed x6, waiting for transfers between devices: 0.1 us -> 62.7 us
    dynamic_slice x0 -> x5, local copies, waits for them, and re-layouts: none -> 43.5 us  [the longest x2 17 us: per_device(): mine = lax.dynamic_index_in_dim(terms, gx, axis=1, keepdims=False)]
    all_to_all x0 -> x3, waiting for transfers between devices: none -> 40 us  [the longest x1 36.4 us: per_device(): lax.all_to_all(reduced.reshape(parts, share, cols), 'gy', 0, 0, tiled=True)]
    ppermute x0 -> x8, waiting for transfers between devices: none -> 36.2 us  [the longest x2 26.4 us: unroll(): mirrored.append(lax.ppermute(blocks[step], 'gy', perm).T)]
    all_gather x1, waiting for transfers between devices: 0.02 us -> 30.7 us  [per_device(): y_basis_all = lax.all_gather(y_basis, 'gy', axis=0)]
  transfers between devices with their start and end apart: 6 -> 15, of which waited for: 5 -> 8; matrix products, arithmetic and copies ran while one was open for 38% -> 15% of each run, Pallas kernels for 0% -> 12%
where the time goes in v1:
time: 518 us; the launch traced here: 517 us
  waiting for transfers between devices  284 us (55%)
  Pallas kernels  89.9 us (17%)
  local copies, waits for them, and re-layouts  69.9 us (13%)
  other arithmetic  35.7 us (7%)
  starting transfers between devices  18.5 us (4%)
  between operations  14 us (3%)
    psum x1, waiting for transfers between devices, per_device(): packed = lax.psum(packed, 'gz') / (total_y * total_slices)  115 us
    unnamed x6, waiting for transfers between devices  62.7 us
    all_to_all x1, waiting for transfers between devices, per_device(): lax.all_to_all(reduced.reshape(parts, share, cols), 'gy', 0, 0, tiled=True)  36.4 us
    pallas_call x1, Pallas kernels, same_half(): pl.pallas_call(functools.partial(same_half_kernel, parts), grid=(slices,)...  33.9 us
    all_gather x1, waiting for transfers between devices, per_device(): y_basis_all = lax.all_gather(y_basis, 'gy', axis=0)  30.7 us
    ppermute x2, waiting for transfers between devices, unroll(): mirrored.append(lax.ppermute(blocks[step], 'gy', perm).T)  26.4 us
    pallas_call x1, Pallas kernels, cross(): pl.pallas_call(cross_kernel, grid_spec=pltpu.PrefetchScalarGridSpec(num_s...  25.8 us
    pallas_call x1, Pallas kernels, project(): pl.pallas_call(project_kernel, grid=(slices,), in_specs=[pl.BlockSpec((ra...  18.8 us
  transfers between devices with their start and end apart: 15, of which 8 were waited for; matrix products, arithmetic and copies ran while one was open for 15% of the time, Pallas kernels for 12%

profile of v1, /device:TPU:0, one launch (start us, length us, event | category | flops | bytes accessed | tf_op | source)
XLA Modules:
  0.0 516.7 jit_solution(3352095510147713716)
XLA Ops:
  7.2 1.6 copy.29
  8.8 0.3 fusion.3.u_ref
  9.0 18.8 %shard_map.60 = (f32[12,128,512]{2,1,0:T(8,128)}, f32[12,128,512]{2,1,0:T(8,128)}) custom-call(f32[256,1024]{1,0:T(8,128)S(1)} %fusion.3.u_ref, f32[12,1024,512]{2,1,0:T(8,128)} %x_ref.3), custom_call_target="tpu_custom_call" | custom-call | flops 9663676416 | bytes 31457280 | tf_op jit(solution)/shard_map/pallas_call | solution.py:41
  27.8 0.5 collective-permute-start.4
  28.3 5.5 %collective-permute-done.4 = f32[12,128,512]{2,1,0:T(8,128)S(1)} collective-permute-done((f32[12,128,512]{2,1,0:T(8,128)}, f32[12,128,512]{2,1,0:T(8,128)S(1)}, u32[]{:S(2)}, u32[]{:S(2)}) %collective-permute-start.4) | collective-permute-done | bytes 3145760 | tf_op jit(solution)/shard_map/ppermute | solution.py:182
  33.8 4.3 add.65
  38.1 5.1 all-to-all-start.1
  43.2 36.4 %all-to-all-done.1.y_ref = f32[4,384,512]{2,1,0:T(8,128)S(1)} async-done(((f32[4,384,512]{2,1,0:T(8,128)}), f32[4,384,512]{2,1,0:T(8,128)S(1)}, u32[]{:S(2)}, u32[]{:S(2)}) %all-to-all-start.1) | async-done | bytes 3145760 | tf_op jit(solution)/shard_map/all_to_all | solution.py:213
  79.6 11.4 %shard_map.61 = f32[4,512,1536]{2,1,0:T(8,128)} custom-call(f32[4,384,512]{2,1,0:T(8,128)S(1)} %all-to-all-done.1.y_ref), custom_call_target="tpu_custom_call" | custom-call | flops 7247757312 | bytes 15728640 | tf_op jit(solution)/shard_map/pallas_call | solution.py:165
  91.0 10.5 %constant_dynamic-slice_fusion.1 = (f32[4,1,256,1536]{3,2,1,0:T(8,128)}, f32[4,1,256,1536]{3,2,1,0:T(8,128)}) fusion(f32[4,2,256,1536]{3,2,1,0:T(8,128)} %bitcast.41, s32[]{:T(128)S(6)} %select_n.78, s32[]{:T(128)S(6)} %select_n.79), kind=kLoop, calls=%fused_computation.31 | loop fusion | bytes 25165832 | tf_op jit(solution)/shard_map/jit(dynamic_index_in_dim)/dynamic_slice | solution.py:230
  101.5 6.6 %copy.31 = f32[4,1,256,1536]{2,3,0,1:T(8,128)} copy(f32[4,1,256,1536]{3,2,1,0:T(8,128)} %get-tuple-element.16) | data formatting | bytes 12582912 | tf_op jit(solution)/shard_map/jit(dynamic_index_in_dim)/dynamic_slice | solution.py:231
  108.1 12.1 %constant_dynamic-slice_fusion.4 = f32[6,1024,512]{2,1,0:T(8,128)} fusion(f32[12,1024,512]{2,1,0:T(8,128)} %x_ref.3, s32[]{:T(128)S(6)} %select_n.77), kind=kLoop, calls=%fused_computation.34 | loop fusion | bytes 25165828 | tf_op jit(solution)/shard_map/dynamic_slice | solution.py:210
  120.2 0.5 collective-permute-start
  120.7 6.6 %copy.30 = f32[4,1,256,1536]{2,3,0,1:T(8,128)} copy(f32[4,1,256,1536]{3,2,1,0:T(8,128)} %get-tuple-element.15) | data formatting | bytes 12582912 | tf_op jit(solution)/shard_map/jit(dynamic_index_in_dim)/dynamic_slice | solution.py:230
  127.3 8.0 %bitcast_add_fusion = f32[4,256,1536]{1,2,0:T(8,128)} fusion(f32[4,256,1536]{1,2,0:T(8,128)} %collective-permute-done.5, f32[4,1,256,1536]{2,3,0,1:T(8,128)} %copy.30), kind=kLoop, calls=%fused_computation.4 | loop fusion | flops 1572864 | bytes 18874368 | tf_op jit(solution)/shard_map/add | solution.py:232
  135.3 0.0 reduce-scatter.9.cloned.1.call-update
  135.3 0.2 reduce-scatter.7.cloned.1.call-start
  135.5 4.3 collective-permute-done.other_ref
  139.8 25.8 %shard_map.59 = f32[1024,1024]{1,0:T(8,128)} custom-call(s32[1]{0:T(128)} %bitcast.gx_ref, f32[12,1024,512]{2,1,0:T(8,128)} %x_ref.3, f32[6,1024,512]{2,1,0:T(8,128)} %collective-permute-done.other_ref), custom_call_target="tpu_custom_call" | custom-call | flops 19327352832 | bytes 25165824 | tf_op jit(solution)/shard_map/pallas_call | solution.py:123
  165.6 6.6 %reshape.33 = f32[4,256,2,512]{3,2,1,0:T(2,128)} reshape(f32[1024,1024]{1,0:T(8,128)} %shard_map.59) | data formatting | bytes 8388608 | tf_op jit(solution)/shard_map/reshape | solution.py:220
  172.2 7.8 %constant_dynamic-slice_fusion.3 = (f32[4,256,1,512]{3,2,1,0:T(1,128)S(1)}, f32[4,256,1,512]{3,2,1,0:T(1,128)S(1)}) fusion(f32[4,256,2,512]{3,2,1,0:T(2,128)} %reshape.33, s32[]{:T(128)S(6)} %select_n.78, s32[]{:T(128)S(6)} %select_n.79), kind=kLoop, calls=%fused_computation.33 | loop fusion | bytes 8388616 | tf_op jit(solution)/shard_map/jit(dynamic_index_in_dim)/dynamic_slice | solution.py:221
  179.9 0.2 copy.49
  180.2 0.5 collective-permute-start.1
  180.7 33.9 %shard_map.58 = f32[4,256,768]{2,1,0:T(8,128)S(1)} custom-call(f32[12,1024,512]{2,1,0:T(8,128)} %x_ref.3), custom_call_target="tpu_custom_call" | custom-call | flops 28991029248 | bytes 25165824 | tf_op jit(solution)/shard_map/pallas_call | solution.py:82
  214.6 0.5 bitcast_add_fusion.1
  215.1 2.8 pad_maximum_fusion
  217.9 0.0 reduce-scatter.7.cloned.1.call-update
  217.9 0.0 all-reduce.5.cloned.1.call-start
  217.9 0.0 reduce-scatter.9.cloned.1.call-done
  218.0 62.1 %reduce-scatter.7.cloned.1.call-done = f32[1,256,1280]{2,1,0:T(8,128)} async-done(((f32[4,256,1280]{2,1,0:T(8,128)}), f32[1,256,1280]{2,1,0:T(8,128)}) %reduce-scatter.7.cloned.1.call-update) | async-done | bytes 1310736
  280.1 0.0 all-reduce.5.cloned.1.call-update
  280.1 0.0 all-gather.3.cloned.1.call-start
  280.2 0.5 all-gather.3.cloned.1.call-update
  280.7 114.8 %all-reduce.5.cloned.1.call-done = (f32[256,1280]{1,0:T(8,128)}, f32[256,1536]{0,1:T(8,128)}) async-done(((f32[256,1280]{1,0:T(8,128)}, f32[256,1536]{0,1:T(8,128)}), (f32[256,1280]{1,0:T(8,128)}, f32[256,1536]{0,1:T(8,128)})) %all-reduce.5.cloned.1.call-update) | async-done | bytes 2883600 | tf_op jit(solution)/shard_map/psum | solution.py:225
  395.5 2.8 broadcast_multiply_fusion
  398.3 0.1 broadcast_multiply_fusion.1
  398.4 1.0 copy-done
  399.5 0.9 slice.29
  400.4 0.5 collective-permute-start.3
  400.9 30.7 %all-gather.3.cloned.1.call-done = f32[2048,256]{1,0:T(8,128)} async-done(((f32[512,256]{1,0:T(8,128)}), f32[2048,256]{1,0:T(8,128)}) %all-gather.3.cloned.1.call-update) | async-done | bytes 2097168 | tf_op jit(solution)/shard_map/all_gather | solution.py:214
  431.6 4.2 fusion.8
  435.8 3.5 all-to-all-start.2
  439.2 1.1 copy.51
  440.3 1.1 copy.50
  441.4 1.1 fusion.7
  442.5 3.6 all-to-all-done.2
  446.1 4.2 all-to-all-start
  450.4 3.6 maximum_select_fusion
  454.0 0.0 slice-start
  454.0 1.0 slice.30
  455.1 2.6 copy.42
  457.6 2.0 collective-permute-start.7
  459.6 0.9 copy.41
  460.4 1.5 collective-permute-start.2
  461.9 1.3 copy.34
  463.1 1.0 reshape.38
  464.1 2.0 copy.36
  466.1 26.4 %collective-permute-done.2 = f32[256,256]{0,1:T(8,128)} collective-permute-done((f32[256,256]{0,1:T(8,128)}, f32[256,256]{0,1:T(8,128)}, u32[]{:S(2)}, u32[]{:S(2)}) %collective-permute-start.2) | collective-permute-done | bytes 262176 | tf_op jit(solution)/shard_map/ppermute | solution.py:192
  492.5 2.3 fusion.6
  494.8 2.8 maximum_select_fusion.2
  497.5 2.5 copy.38
  500.1 3.9 maximum_select_fusion.1
  503.9 3.3 fusion.2
  507.3 2.9 copy.35
  (17 shorter events, 0.0 us)
Async XLA Ops:
  27.8 6.0 %collective-permute-start.4 = (f32[12,128,512]{2,1,0:T(8,128)}, f32[12,128,512]{2,1,0:T(8,128)S(1)}, u32[]{:S(2)}, u32[]{:S(2)}) collective-permute-start(f32[12,128,512]{2,1,0:T(8,128)} %get-tuple-element.6), channel_id=1, source_target_pairs={{0,16},{16,0},{1,17},{17,1},{2,18},{18,2},{3,19},{19,3},{4,20},{20... | collective-permute-start | bytes 9437192 | tf_op jit(solution)/shard_map/ppermute | solution.py:182
  38.1 41.5 %all-to-all-start.1 = ((f32[4,384,512]{2,1,0:T(8,128)}), f32[4,384,512]{2,1,0:T(8,128)S(1)}, u32[]{:S(2)}, u32[]{:S(2)}) async-start(f32[4,384,512]{2,1,0:T(8,128)} %bitcast.42), calls=%async_computation.1 | async-start | bytes 6291456 | tf_op jit(solution)/shard_map/all_to_all | solution.py:213
  43.2 174.8 %reduce-scatter.9.cloned.1.call-start = ((), (), s32[]{:S(2)}) async-start(), calls=%async_computation.7 | async-start | bytes 7864320
  108.1 19.2 %collective-permute-start.5 = (f32[4,256,1536]{1,2,0:T(8,128)}, f32[4,256,1536]{1,2,0:T(8,128)}, u32[]{:S(2)}, u32[]{:S(2)}) collective-permute-start(f32[4,256,1536]{1,2,0:T(8,128)} %bitcast.43), channel_id=1, source_target_pairs={{0,16},{16,0},{1,17},{17,1},{2,18},{18,2},{3,19},{19,3},{4,20},{20... | collective-permute-start | bytes 18874376 | tf_op jit(solution)/shard_map/ppermute | solution.py:182
  120.2 19.6 %collective-permute-start = (f32[6,1024,512]{2,1,0:T(8,128)}, f32[6,1024,512]{2,1,0:T(8,128)}, u32[]{:S(2)}, u32[]{:S(2)}) collective-permute-start(f32[6,1024,512]{2,1,0:T(8,128)} %constant_dynamic-slice_fusion.4), channel_id=1, source_target_pairs={{0,16},{16,0},{1,17},{17,1},{2,18},{18,2},{3,19},{19,3},{4,20},{20... | collective-permute-start | bytes 37748744 | tf_op jit(solution)/shard_map/ppermute | solution.py:182
  135.3 144.8 %reduce-scatter.7.cloned.1.call-start = ((), (), s32[]{:S(2)}) async-start(), calls=%async_computation.6 | async-start | bytes 6553600
  180.2 34.4 %collective-permute-start.1 = (f32[4,256,512]{2,1,0:T(8,128)S(1)}, f32[4,256,512]{2,1,0:T(8,128)S(1)}, u32[]{:S(2)}, u32[]{:S(2)}) collective-permute-start(f32[4,256,512]{2,1,0:T(8,128)S(1)} %bitcast.48), channel_id=1, source_target_pairs={{0,16},{16,0},{1,17},{17,1},{2,18},{18,2},{3,19},{19,3},{4,20},{20... | collective-permute-start | bytes 6291464 | tf_op jit(solution)/shard_map/ppermute | solution.py:182
  217.9 177.6 %all-reduce.5.cloned.1.call-start = ((), (), s32[]{:S(2)}) async-start(), calls=%async_computation.8 | async-start | bytes 5767168 | tf_op jit(solution)/shard_map/psum | solution.py:225
  280.1 151.4 %all-gather.3.cloned.1.call-start = ((), (), s32[]{:S(2)}) async-start(), calls=%async_computation.5 | async-start | bytes 2621440 | tf_op jit(solution)/shard_map/all_gather | solution.py:214
  395.5 2.8 copy-start.2
  398.3 52.0 %collective-permute-start.6 = (f32[256,1536]{0,1:T(8,128)}, f32[256,1536]{0,1:T(8,128)}, u32[]{:S(2)}, u32[]{:S(2)}) collective-permute-start(f32[256,1536]{0,1:T(8,128)} %broadcast_multiply_fusion), channel_id=1, source_target_pairs={{0,16},{16,0},{1,17},{17,1},{2,18},{18,2},{3,19},{19,3},{4,20},{20... | collective-permute-start | bytes 4718600 | tf_op jit(solution)/shard_map/ppermute | solution.py:182
  398.4 1.1 copy-start
  400.4 40.0 %collective-permute-start.3 = (f32[256,512]{1,0:T(8,128)}, f32[256,512]{1,0:T(8,128)}, u32[]{:S(2)}, u32[]{:S(2)}) collective-permute-start(f32[256,512]{1,0:T(8,128)} %slice.29), channel_id=1, source_target_pairs={{0,16},{16,0},{1,17},{17,1},{2,18},{18,2},{3,19},{19,3},{4,20},{20... | collective-permute-start | bytes 1572872 | tf_op jit(solution)/shard_map/ppermute | solution.py:182
  435.8 10.3 %all-to-all-start.2 = ((f32[4,384,64]{1,2,0:T(8,128)}), f32[4,384,64]{1,2,0:T(8,128)S(1)}, u32[]{:S(2)}, u32[]{:S(2)}) async-start(f32[4,384,64]{1,2,0:T(8,128)} %bitcast.16), calls=%async_computation.2 | async-start | bytes 786432 | tf_op jit(solution)/shard_map/all_to_all | solution.py:237
  446.1 4.3 copy-start.1
  446.1 51.5 %all-to-all-start = ((f32[4,256,256]{1,2,0:T(8,128)}), f32[4,256,256]{1,2,0:T(8,128)}, u32[]{:S(2)}, u32[]{:S(2)}) async-start(f32[4,256,256]{1,2,0:T(8,128)} %fusion.7), calls=%async_computation | async-start | bytes 2097152 | tf_op jit(solution)/shard_map/all_to_all | solution.py:251
  454.0 5.6 %slice-start = ((f32[256,1280]{1,0:T(8,128)}), f32[256,256]{1,0:T(8,128)S(1)}, s32[]{:S(2)}) async-start(f32[256,1280]{1,0:T(8,128)} %copy-done), calls=%async_computation.9 | async-start | bytes 524288 | tf_op jit(solution)/shard_map/slice | solution.py:187
  457.6 46.3 %collective-permute-start.7 = (f32[512,512]{1,0:T(8,128)}, f32[512,512]{1,0:T(8,128)}, u32[]{:S(2)}, u32[]{:S(2)}) collective-permute-start(f32[512,512]{1,0:T(8,128)} %copy.42), channel_id=1, source_target_pairs={{0,4},{4,8},{8,12},{12,0},{1,5},{5,9},{9,13},{13,1},{2,6},{6,10},{... | collective-permute-start | bytes 3145736 | tf_op jit(solution)/shard_map/ppermute | solution.py:192
  460.4 32.0 %collective-permute-start.2 = (f32[256,256]{0,1:T(8,128)}, f32[256,256]{0,1:T(8,128)}, u32[]{:S(2)}, u32[]{:S(2)}) collective-permute-start(f32[256,256]{0,1:T(8,128)} %copy.41), channel_id=1, source_target_pairs={{0,4},{4,8},{8,12},{12,0},{1,5},{5,9},{9,13},{13,1},{2,6},{6,10},{... | collective-permute-start | bytes 786440 | tf_op jit(solution)/shard_map/ppermute | solution.py:192
  464.1 28.4 %slice-start.1 = ((f32[256,1280]{1,0:T(8,128)}), f32[256,768]{1,0:T(8,128)S(1)}, s32[]{:S(2)}) async-start(f32[256,1280]{1,0:T(8,128)} %copy-done), calls=%async_computation.10 | async-start | bytes 1572864 | tf_op jit(solution)/shard_map/slice | solution.py:187
Sparse Core Ops, SparseCore 0:
  135.4 70.7 reduce-scatter.8
  218.0 62.0 reduce-scatter.6
  282.6 112.9 all-reduce.4
  397.2 34.3 all-gather.2

commit v2 on v1

v2 whole, which is shorter than its diff:
```python
import functools

import jax
import jax.numpy as jnp
from jax import lax
from jax.experimental import pallas as pl
from jax.experimental.pallas import tpu as pltpu
from jax.sharding import PartitionSpec as P

F32, BF16 = jnp.float32, jnp.bfloat16
LIMIT = 50 * 2**20
MESH = pl.DeviceIdType.MESH


def split(x):
    hi = x.astype(BF16)
    return hi, (x - hi.astype(F32)).astype(BF16)


def dot(a, b, dims):
    return lax.dot_general(a, b, (dims, ((), ())), preferred_element_type=F32)


def project_kernel(u_ref, x_ref, keep_ref, send_ref):
    u_hi, u_lo = split(u_ref[...])
    x_hi, x_lo = split(x_ref[0])
    out = dot(
        jnp.concatenate([u_hi, u_hi, u_lo], axis=1),
        jnp.concatenate([x_hi, x_lo, x_hi], axis=0),
        ((1,), (0,)),
    )
    half = keep_ref.shape[1]
    keep_ref[0] = out[:half]
    send_ref[0] = out[half:]


def project(field, basis):
    slices, rows, cols = field.shape
    rank = basis.shape[0]
    out = jax.ShapeDtypeStruct((slices, rank // 2, cols), F32)
    block = pl.BlockSpec((1, rank // 2, cols), lambda s: (s, 0, 0))
    return pl.pallas_call(
        project_kernel,
        grid=(slices,),
        in_specs=[
            pl.BlockSpec((rank, rows), lambda s: (0, 0)),
            pl.BlockSpec((1, rows, cols), lambda s: (s, 0, 0)),
        ],
        out_specs=[block, block],
        out_shape=[out, out],
        compiler_params=pltpu.CompilerParams(vmem_limit_bytes=LIMIT),
        cost_estimate=pl.CostEstimate(
            flops=6 * slices * rows * cols * rank,
            bytes_accessed=4 * slices * cols * (rows + rank),
            transcendentals=0,
        ),
    )(basis, field)


def same_half_kernel(parts, x_ref, field_ref, out_ref, other_ref, a_ref, b_ref, send_sem, recv_sem):
    rows, cols = x_ref.shape[1:]
    b = rows // parts
    wide = out_ref.shape[2]
    half = other_ref.shape[0]
    gx = lax.axis_index("gx")
    step = pl.program_id(0)
    copy = pltpu.make_async_remote_copy(
        src_ref=field_ref.at[pl.ds((1 - gx) * half, half)],
        dst_ref=other_ref,
        send_sem=send_sem,
        recv_sem=recv_sem,
        device_id={"gx": 1 - gx},
        device_id_type=MESH,
    )

    @pl.when(step == 0)
    def _():
        barrier = pltpu.get_barrier_semaphore()
        pl.semaphore_signal(barrier, inc=1, device_id={"gx": 1 - gx}, device_id_type=MESH)
        pl.semaphore_wait(barrier, 1)
        copy.start()
        out_ref[...] = jnp.zeros_like(out_ref)

    hi, lo = split(x_ref[0])
    for n, v in enumerate((hi, hi, lo)):
        a_ref[:, n * cols : (n + 1) * cols] = v
    for n, v in enumerate((hi, lo, hi)):
        b_ref[:rows, n * cols : (n + 1) * cols] = v
        b_ref[rows:, n * cols : (n + 1) * cols] = v[: b_ref.shape[0] - rows]
    for i in range(parts):
        out_ref[i] += dot(a_ref[i * b : (i + 1) * b], b_ref[i * b : i * b + wide], ((1,), (1,)))

    @pl.when(step == pl.num_programs(0) - 1)
    def _():
        copy.wait()


def same_half(field, parts):
    slices, rows, cols = field.shape
    b = rows // parts
    wide = b * (parts // 2 + 1)
    return pl.pallas_call(
        functools.partial(same_half_kernel, parts),
        grid=(slices,),
        in_specs=[
            pl.BlockSpec((1, rows, cols), lambda s: (s, 0, 0)),
            pl.BlockSpec(memory_space=pl.ANY),
        ],
        out_specs=[
            pl.BlockSpec((parts, b, wide), lambda s: (0, 0, 0)),
            pl.BlockSpec(memory_space=pl.ANY),
        ],
        out_shape=[
            jax.ShapeDtypeStruct((parts, b, wide), F32),
            jax.ShapeDtypeStruct((slices // 2, rows, cols), F32),
        ],
        scratch_shapes=[
            pltpu.VMEM((rows, 3 * cols), BF16),
            pltpu.VMEM((rows + wide - b, 3 * cols), BF16),
            pltpu.SemaphoreType.DMA,
            pltpu.SemaphoreType.DMA,
        ],
        compiler_params=pltpu.CompilerParams(
            collective_id=2, has_side_effects=True, vmem_limit_bytes=LIMIT
        ),
        cost_estimate=pl.CostEstimate(
            flops=6 * slices * rows * cols * wide,
            bytes_accessed=4 * slices * cols * rows,
            transcendentals=0,
        ),
    )(field, field)


def cross_kernel(gx_ref, own_ref, other_ref, keep_ref, send_ref, a_ref, b_ref):
    rows, cols = own_ref.shape[1:]

    @pl.when(pl.program_id(0) == 0)
    def _():
        keep_ref[...] = jnp.zeros_like(keep_ref)
        send_ref[...] = jnp.zeros_like(send_ref)

    first = gx_ref[0] == 0
    own, other = own_ref[0], other_ref[0]
    hi, lo = split(jnp.where(first, own, other))
    for n, v in enumerate((hi, hi, lo)):
        a_ref[:, n * cols : (n + 1) * cols] = v
    hi, lo = split(jnp.where(first, other, own))
    for n, v in enumerate((hi, lo, hi)):
        b_ref[:, n * cols : (n + 1) * cols] = v
    parts, b, half = keep_ref.shape
    for ref, g in ((keep_ref, gx_ref[0]), (send_ref, 1 - gx_ref[0])):
        right = b_ref[pl.ds(pl.multiple_of(g * half, half), half)]
        for i in range(parts):
            ref[i] += dot(a_ref[i * b : (i + 1) * b], right, ((1,), (1,)))


def cross(gx, field, other, parts):
    slices, rows, cols = other.shape
    shape = (parts, rows // parts, rows // 2)
    return pl.pallas_call(
        cross_kernel,
        grid_spec=pltpu.PrefetchScalarGridSpec(
            num_scalar_prefetch=1,
            grid=(slices,),
            in_specs=[
                pl.BlockSpec((1, rows, cols), lambda s, g: (g[0] * slices + s, 0, 0)),
                pl.BlockSpec((1, rows, cols), lambda s, g: (s, 0, 0)),
            ],
            out_specs=[pl.BlockSpec(shape, lambda s, g: (0, 0, 0))] * 2,
            scratch_shapes=[pltpu.VMEM((rows, 3 * cols), BF16)] * 2,
        ),
        out_shape=[jax.ShapeDtypeStruct(shape, F32)] * 2,
        compiler_params=pltpu.CompilerParams(vmem_limit_bytes=LIMIT),
        cost_estimate=pl.CostEstimate(
            flops=6 * slices * rows * cols * rows,
            bytes_accessed=8 * slices * cols * rows,
            transcendentals=0,
        ),
    )(jnp.reshape(gx, (1,)).astype(jnp.int32), field, other)


def gram_y_kernel(gx_ref, y_ref, keep_ref, send_ref, b_ref):
    parts, depth, cols = y_ref.shape
    wide = keep_ref.shape[2]
    i = pl.program_id(0)

    @pl.when(i == 0)
    def _():
        for j in range(b_ref.shape[1] // cols):
            hi, lo = split(y_ref[j % parts])
            b_ref[:, j * cols : (j + 1) * cols] = jnp.concatenate([hi, lo, hi], axis=0)

    hi, lo = split(jnp.transpose(y_ref[i]))
    a = jnp.concatenate([hi, hi, lo], axis=1)
    start = pl.multiple_of(i * cols, cols)
    out = dot(a, b_ref[:, pl.ds(start, wide)], ((1,), (0,)))

    @pl.when(gx_ref[0] == 0)
    def _():
        keep_ref[0] = out[: cols // 2]
        send_ref[0] = out[cols // 2 :]

    @pl.when(gx_ref[0] == 1)
    def _():
        keep_ref[0] = out[cols // 2 :]
        send_ref[0] = out[: cols // 2]


def gram_y_terms(gx, y):
    parts, depth, cols = y.shape
    wide = cols * (parts // 2 + 1)
    return pl.pallas_call(
        gram_y_kernel,
        grid_spec=pltpu.PrefetchScalarGridSpec(
            num_scalar_prefetch=1,
            grid=(parts,),
            in_specs=[pl.BlockSpec((parts, depth, cols), lambda i, g: (0, 0, 0))],
            out_specs=[pl.BlockSpec((1, cols // 2, wide), lambda i, g: (i, 0, 0))] * 2,
            scratch_shapes=[pltpu.VMEM((3 * depth, parts * cols + wide - cols), BF16)],
        ),
        out_shape=[jax.ShapeDtypeStruct((parts, cols // 2, wide), F32)] * 2,
        compiler_params=pltpu.CompilerParams(vmem_limit_bytes=LIMIT),
        cost_estimate=pl.CostEstimate(
            flops=6 * parts * depth * cols * wide,
            bytes_accessed=4 * parts * cols * (wide + depth),
            transcendentals=0,
        ),
    )(jnp.reshape(gx, (1,)).astype(jnp.int32), y)


def spread(m, bits):
    return sum(((m >> (len(bits) - 1 - j)) & 1) << k for j, k in enumerate(bits))


def reduce_kernel(parts, planes, pieces, *refs):
    n = len(pieces)
    given = [a for a in range(n) if pieces[a][2]]
    g = len(given)
    ins, sends, outs, refs = refs[:n], refs[n : n + g], refs[n + g : 2 * n + g], refs[2 * n + g :]
    sends, partner = dict(zip(given, sends)), dict(zip(given, refs[:g]))
    refs = refs[g:]
    nbits = parts.bit_length() - 1
    steps = [refs[t * n : (t + 1) * n] for t in range(nbits)]
    z_in, z_mid, z_out = (refs[t * n : (t + 1) * n] for t in range(nbits, nbits + 3))
    send_sem, recv_sem = refs[(nbits + 3) * n :]
    gx, gy, gz = lax.axis_index("gx"), lax.axis_index("gy"), lax.axis_index("gz")
    terms = [partner.get(a, ins[a]) for a in range(n)]
    bit = [(gy // 2**k) % 2 for k in range(nbits)]
    side = gz // (planes // 2)
    depth = gz + side * (planes - 1 - 2 * gz)
    inward, outward = gz + 1 - 2 * side, gz - 1 + 2 * side
    middle = planes // 2 - 1

    chunks = []
    for a, (h, count, _) in enumerate(pieces):
        for c in range(count):
            rows = pl.ds(c * (h // count), h // count)
            order = list(range(nbits)) if c % 2 else list(range(nbits))[::-1]
            chunks.append((a, rows, order))

    barrier = pltpu.get_barrier_semaphore()
    for k in range(nbits):
        pl.semaphore_signal(
            barrier, inc=1, device_id={"gy": gy + (1 - 2 * bit[k]) * 2**k}, device_id_type=MESH
        )
    pl.semaphore_signal(barrier, inc=1, device_id={"gx": 1 - gx}, device_id_type=MESH)
    pl.semaphore_signal(barrier, inc=1, device_id={"gz": inward}, device_id_type=MESH)

    @pl.when(depth > 0)
    def _():
        pl.semaphore_signal(barrier, inc=1, device_id={"gz": outward}, device_id_type=MESH)

    pl.semaphore_wait(barrier, nbits + 2 + (depth + planes - 1) // planes)

    def across(c):
        a, rows, order = chunks[c]
        slot = parts // 2 + nbits + 2
        return pltpu.make_async_remote_copy(
            src_ref=sends[a].at[:, rows],
            dst_ref=partner[a].at[:, rows],
            send_sem=send_sem.at[c, slot],
            recv_sem=recv_sem.at[c, slot],
            device_id={"gx": 1 - gx},
            device_id_type=MESH,
        )

    def first(c):
        a, rows, order = chunks[c]
        if a in given:
            across(c).wait_recv()
            for m in range(parts):
                partner[a][m, rows] += ins[a][m, rows]
        for copy in halving(0, c):
            copy.start()

    def halving(t, c):
        a, rows, order = chunks[c]
        k = order[t]
        to = {"gy": gy + (1 - 2 * bit[k]) * 2**k}
        left = 2 ** (nbits - 1 - t)
        if t == 0:
            base = (1 - bit[k]) * 2**k
            return [
                pltpu.make_async_remote_copy(
                    src_ref=terms[a].at[base + spread(m, order[1:]), rows],
                    dst_ref=steps[0][a].at[m, rows],
                    send_sem=send_sem.at[c, m],
                    recv_sem=recv_sem.at[c, m],
                    device_id=to,
                    device_id_type=MESH,
                )
                for m in range(left)
            ]
        slot = parts // 2 + t - 1
        return [
            pltpu.make_async_remote_copy(
                src_ref=steps[t - 1][a].at[pl.ds((1 - bit[k]) * left, left), rows],
                dst_ref=steps[t][a].at[:, rows],
                send_sem=send_sem.at[c, slot],
                recv_sem=recv_sem.at[c, slot],
                device_id=to,
                device_id_type=MESH,
            )
        ]

    def along_z(c, kind):
        a, rows, order = chunks[c]
        slot = parts // 2 + nbits - 1 + kind
        total = steps[nbits - 1][a].at[0, rows]
        src = (total, total, z_out[a].at[rows])[kind]
        dst = (z_in, z_mid, z_out)[kind][a].at[rows]
        return pltpu.make_async_remote_copy(
            src_ref=src,
            dst_ref=dst,
            send_sem=send_sem.at[c, slot],
            recv_sem=recv_sem.at[c, slot],
            device_id={"gz": outward if kind == 2 else inward},
            device_id_type=MESH,
        )

    def stage(t, c):
        a, rows, order = chunks[c]
        if t < nbits:
            for copy in halving(t, c):
                copy.wait_recv()
            k = order[t]
            left = 2 ** (nbits - 1 - t)
            for m in range(left):
                if t == 0:
                    own = terms[a][bit[k] * 2**k + spread(m, order[1:]), rows]
                else:
                    own = steps[t - 1][a][bit[k] * left + m, rows]
                steps[t][a][m, rows] += own
            if t + 1 < nbits:
                for copy in halving(t + 1, c):
                    copy.start()
            else:
                @pl.when((depth == 0) if middle > 0 else (depth > planes))
                def _():
                    along_z(c, 0).start()

        elif t == nbits:
            @pl.when(depth > 0)
            def _():
                along_z(c, 0).wait_recv()
                steps[nbits - 1][a][0, rows] += z_in[a][rows]

            @pl.when(depth == middle)
            def _():
                along_z(c, 1).start()

            if middle > 1:
                @pl.when((depth > 0) & (depth < middle))
                def _():
                    along_z(c, 0).start()

        else:
            @pl.when(depth == middle)
            def _():
                along_z(c, 1).wait_recv()
                z_out[a][rows] = steps[nbits - 1][a][0, rows] + z_mid[a][rows]

            @pl.when(depth < middle)
            def _():
                along_z(c, 2).wait_recv()

            @pl.when(depth > 0)
            def _():
                along_z(c, 2).start()

            outs[a][rows] = z_out[a][rows]

    for c in range(len(chunks)):
        if chunks[c][0] in given:
            across(c).start()
    stages, ahead = nbits + 2, 3
    for c in range(ahead):
        first(c)
    for tick in range(len(chunks) + stages - 1):
        if tick + ahead < len(chunks):
            first(tick + ahead)
        for t in range(stages):
            if 0 <= tick - t < len(chunks):
                stage(t, tick - t)
    for c in range(len(chunks)):
        if chunks[c][0] in given:
            across(c).wait_send()
        for t in range(nbits):
            for copy in halving(t, c):
                copy.wait_send()

        @pl.when(depth < middle)
        def _():
            along_z(c, 0).wait_send()

        @pl.when(depth == middle)
        def _():
            along_z(c, 1).wait_send()

        @pl.when(depth > 0)
        def _():
            along_z(c, 2).wait_send()


def reduce_all(arrays, sends, parts, planes, counts, collective_id):
    pieces = [(x.shape[1], n, y is not None) for x, y, n in zip(arrays, sends, counts)]
    sends = [y for y in sends if y is not None]
    size = sum(x.size for x in arrays)
    nbits = parts.bit_length() - 1
    slots = parts // 2 + nbits + 3
    sems = pltpu.SemaphoreType.DMA((sum(counts), slots))
    vmem = pl.BlockSpec(memory_space=pltpu.VMEM)
    return pl.pallas_call(
        functools.partial(reduce_kernel, parts, planes, pieces),
        in_specs=[vmem] * len(arrays) + [pl.BlockSpec(memory_space=pl.ANY)] * len(sends),
        out_specs=[vmem] * len(arrays),
        out_shape=[jax.ShapeDtypeStruct(x.shape[1:], F32) for x in arrays],
        scratch_shapes=[pltpu.VMEM(x.shape, F32) for x in sends]
        + [
            pltpu.VMEM((parts // 2 ** (t + 1),) + x.shape[1:], F32) for t in range(nbits) for x in arrays
        ]
        + [pltpu.VMEM(x.shape[1:], F32) for x in arrays] * 3
        + [sems, sems],
        compiler_params=pltpu.CompilerParams(
            collective_id=collective_id, has_side_effects=True, vmem_limit_bytes=58 * 2**20
        ),
        cost_estimate=pl.CostEstimate(
            flops=2 * size, bytes_accessed=4 * size, transcendentals=0
        ),
    )(*arrays, *sends)


def swap(x, axis_name):
    return lax.ppermute(x, axis_name, [(0, 1), (1, 0)])


def mirror(block, step, parts):
    perm = [(i, (i + step) % parts) for i in range(parts)]
    return lax.ppermute(block, "gy", perm).T


def unroll(piece, gy, parts):
    b = piece.shape[1] // (parts // 2 + 1)
    blocks = [piece[:, k * b : (k + 1) * b] for k in range(parts // 2 + 1)]
    mirrored = [mirror(blocks[step], step, parts) for step in range(parts // 2 - 1, 0, -1)]
    return pick(blocks + mirrored, [(j + parts - gy) % parts for j in range(parts)])


def pick(blocks, places):
    stack = jnp.stack(blocks)
    return jnp.concatenate(
        [lax.dynamic_index_in_dim(stack, k, axis=0, keepdims=False) for k in places], axis=1
    )


def per_device(field, x_basis, y_basis):
    gx, gy = lax.axis_index("gx"), lax.axis_index("gy")
    parts, planes = lax.axis_size("gy"), lax.axis_size("gz")
    slices, rows, cols = field.shape
    rank = x_basis.shape[1]
    total_y, total_slices = cols * parts, slices * planes
    half = slices // 2

    basis = jnp.roll(x_basis.T, -gx * (rank // 2), axis=0)
    keep, send = project(field, basis)
    reduced = keep + swap(send, "gx")

    share = slices * (rank // 2) // parts
    y_basis_all = lax.all_gather(y_basis, "gy", axis=0)

    reduced, field = lax.optimization_barrier((reduced, field))
    y_rows = lax.all_to_all(reduced.reshape(parts, share, cols), "gy", 0, 0, tiled=True)
    same, other = same_half(field, parts)
    keep_x, send_x = cross(gx, field, other, parts)
    y_rows, same = lax.optimization_barrier((y_rows, same))
    keep_y, send_y = gram_y_terms(gx, y_rows)

    same, across, part_y = reduce_all(
        (same, keep_x, keep_y), (None, send_x, send_y), parts, planes, (4, 4, 4), 1
    )
    same, across = same / (total_y * total_slices), across / (total_y * total_slices)
    part_y = part_y / (rank * total_slices)

    core = jnp.einsum("gkl,glq->kq", y_rows, y_basis_all, precision=lax.Precision.HIGH)
    q = core.shape[1]
    core = lax.all_to_all(
        core.reshape(share, parts, q // parts).transpose(1, 0, 2), "gy", 0, 0, tiled=True
    )
    core = core.reshape(slices, rank // 2, q // parts).transpose(1, 0, 2)

    b = rows // parts
    diagonal = unroll(same, gy, parts)
    mine = across
    theirs = swap(mine, "gx")
    strip = jnp.where(
        gx == 0,
        jnp.concatenate([mine, theirs], axis=1),
        jnp.concatenate([theirs, mine], axis=1),
    )
    columns = lax.all_to_all(
        strip.reshape(b, parts, b).transpose(1, 2, 0), "gy", 0, 0, tiled=True
    )
    columns = columns.transpose(1, 0, 2).reshape(b, rows)
    gram_x = jnp.where(
        gx == 0,
        jnp.concatenate([diagonal, strip], axis=1),
        jnp.concatenate([columns, diagonal], axis=1),
    )

    blocks = [part_y[:, k * cols : (k + 1) * cols] for k in range(parts // 2 + 1)]
    mirrored = [mirror(blocks[step], step, parts) for step in range(parts // 2 - 1, 0, -1)]
    theirs = swap((part_y, mirrored), "gx")
    whole = jnp.where(
        gx == 0,
        jnp.concatenate([part_y, theirs[0]], axis=0),
        jnp.concatenate([theirs[0], part_y], axis=0),
    )
    blocks = [whole[:, k * cols : (k + 1) * cols] for k in range(parts // 2 + 1)]
    for own, got in zip(mirrored, theirs[1]):
        blocks.append(
            jnp.where(
                gx == 0,
                jnp.concatenate([own, got], axis=1),
                jnp.concatenate([got, own], axis=1),
            )
        )
    first = gx * (parts // 2) + parts - gy
    gram_y = pick(blocks, [(first + j) % parts for j in range(parts // 2)])
    return (gram_x, gram_y, core)


def solution(mesh):
    in_specs = (P("gz", "gx", "gy"), P("gx", None), P("gy", None))
    out_specs = (P(("gx", "gy"), None), P("gy", "gx"), P("gx", "gz", "gy"))
    return jax.shard_map(
        per_device, mesh=mesh, in_specs=in_specs, out_specs=out_specs, check_vma=False
    )
```

time: 518 us -> 354 us (0.68)
  waiting for transfers between devices: 284 us -> 28.4 us
  Pallas kernels: 89.9 us -> 256 us
  local copies, waits for them, and re-layouts: 69.9 us -> 16 us
  other arithmetic: 35.7 us -> 19.4 us
    pallas_call x1 -> x2, Pallas kernels: 11.4 us -> 174 us  [the longest x1 162 us: reduce_all(): pl.pallas_call(functools.partial(reduce_kernel, parts, planes, pieces), i...]
    psum x1 -> x0, waiting for transfers between devices: 115 us -> none  [per_device(): packed = lax.psum(packed, 'gz') / (total_y * total_slices)]
    unnamed x6 -> x1, waiting for transfers between devices: 62.7 us -> 0.02 us
    dynamic_slice x5 -> x3, local copies, waits for them, and re-layouts: 43.5 us -> 0.87 us  [pick(): lax.dynamic_index_in_dim(stack, k, axis=0, keepdims=False)]
    all_to_all x1, waiting for transfers between devices: 36.4 us -> 0.01 us  [per_device(): lax.all_to_all(reduced.reshape(parts, share, cols), 'gy', 0, 0, tiled=True)]
    all_gather x1, waiting for transfers between devices: 30.7 us -> 0.01 us  [per_device(): y_basis_all = lax.all_gather(y_basis, 'gy', axis=0)]
    add x2 -> x0, other arithmetic: 8.48 us -> none  [the longest x1 8 us: per_device(): mine + theirs]
    concatenate x3 -> x2, other arithmetic: 8.39 us -> 1.61 us  [the longest x1 1.51 us: pick(): jnp.concatenate([lax.dynamic_index_in_dim(stack, k, axis=0, keepdims=Fals...]
  transfers between devices with their start and end apart: 15 -> 10, of which waited for: 8 -> 3; matrix products, arithmetic and copies ran while one was open for 15% -> 6% of each run, Pallas kernels for 12% -> 67%
where the time goes in v2:
time: 354 us; the launch traced here: 353 us
  Pallas kernels  256 us (72%)
  waiting for transfers between devices  28.4 us (8%)
  other arithmetic  19.4 us (5%)
  local copies, waits for them, and re-layouts  16 us (5%)
  starting transfers between devices  14.7 us (4%)
  between operations  14.3 us (4%)
  matrix products  4.18 us (1%)
    pallas_call x1, Pallas kernels, reduce_all(): pl.pallas_call(functools.partial(reduce_kernel, parts, planes, pieces), i...  162 us
    pallas_call x1, Pallas kernels, same_half(): pl.pallas_call(functools.partial(same_half_kernel, parts), grid=(slices,)...  33.7 us
    pallas_call x1, Pallas kernels, cross(): pl.pallas_call(cross_kernel, grid_spec=pltpu.PrefetchScalarGridSpec(num_s...  29.5 us
    ppermute x2, waiting for transfers between devices, mirror(): return lax.ppermute(block, 'gy', perm).T  22.9 us
    pallas_call x1, Pallas kernels, project(): pl.pallas_call(project_kernel, grid=(slices,), in_specs=[pl.BlockSpec((ra...  18.8 us
    pallas_call x1, Pallas kernels, gram_y_terms(): pl.pallas_call(gram_y_kernel, grid_spec=pltpu.PrefetchScalarGridSpec(num_...  12.3 us
    unnamed x25, local copies, waits for them, and re-layouts  9.47 us
  transfers between devices with their start and end apart: 10, of which 3 were waited for; matrix products, arithmetic and copies ran while one was open for 6% of the time, Pallas kernels for 67%

profile of v2, /device:TPU:0, one launch (start us, length us, event | category | flops | bytes accessed | tf_op | source)
XLA Modules:
  0.0 353.1 jit_solution(8718828180959451296)
XLA Ops:
  7.2 0.0 all-gather.3.cloned.1.call-start
  7.2 1.6 copy.25
  8.8 0.3 fusion.u_ref
  9.1 18.8 %shard_map.58 = (f32[12,128,512]{2,1,0:T(8,128)}, f32[12,128,512]{2,1,0:T(8,128)}) custom-call(f32[256,1024]{1,0:T(8,128)S(1)} %fusion.u_ref, f32[12,1024,512]{2,1,0:T(8,128)} %own_ref), custom_call_target="tpu_custom_call" | custom-call | flops 9663676416 | bytes 31457280 | tf_op jit(solution)/shard_map/pallas_call | solution.py:42
  27.9 0.5 collective-permute-start
  28.4 0.0 all-gather.3.cloned.1.call-update
  28.4 5.5 %collective-permute-done = f32[12,128,512]{2,1,0:T(8,128)S(1)} collective-permute-done((f32[12,128,512]{2,1,0:T(8,128)}, f32[12,128,512]{2,1,0:T(8,128)S(1)}, u32[]{:S(2)}, u32[]{:S(2)}) %collective-permute-start) | collective-permute-done | bytes 3145760 | tf_op jit(solution)/shard_map/ppermute | solution.py:454
  33.9 4.3 %add.60 = f32[12,128,512]{2,1,0:T(8,128)} add(f32[12,128,512]{2,1,0:T(8,128)} %get-tuple-element.18, f32[12,128,512]{2,1,0:T(8,128)S(1)} %collective-permute-done) | non-fusion elementwise | flops 786432 | bytes 9437184 | tf_op jit(solution)/shard_map/add | solution.py:486
  38.2 5.1 %all-to-all-start = ((f32[4,384,512]{2,1,0:T(8,128)}), f32[4,384,512]{2,1,0:T(8,128)S(1)}, u32[]{:S(2)}, u32[]{:S(2)}) async-start(f32[4,384,512]{2,1,0:T(8,128)} %bitcast.59), calls=%async_computation | async-start | bytes 6291456 | tf_op jit(solution)/shard_map/all_to_all | solution.py:492
  43.2 33.7 %shard_map.59 = (f32[4,256,768]{2,1,0:T(8,128)S(1)}, f32[6,1024,512]{2,1,0:T(8,128)}) custom-call(f32[12,1024,512]{2,1,0:T(8,128)} %own_ref, f32[12,1024,512]{2,1,0:T(8,128)} %own_ref), custom_call_target="tpu_custom_call" | custom-call | flops 28991029248 | bytes 25165824 | tf_op jit(solution)/shard_map/pallas_call | solution.py:102
  77.0 1.6 copy-done
  78.6 29.5 %shard_map.60 = (f32[4,256,512]{2,1,0:T(8,128)S(1)}, f32[4,256,512]{2,1,0:T(8,128)}) custom-call(s32[1]{0:T(128)} %bitcast.2.gx_ref, f32[12,1024,512]{2,1,0:T(8,128)} %own_ref, f32[6,1024,512]{2,1,0:T(8,128)} %get-tuple-element.24.other_ref), custom_call_target="tpu_custom_call" | custom-call | flops 19327352832 | bytes 25165824 | tf_op jit(solution)/shard_map/pallas_call | solution.py:160
  108.1 1.3 copy-done.1
  109.4 0.0 all-to-all-done.y_ref
  109.4 12.3 %shard_map.61 = (f32[4,256,1536]{2,1,0:T(8,128)}, f32[4,256,1536]{2,1,0:T(8,128)}) custom-call(s32[1]{0:T(128)} %bitcast.2.gx_ref, f32[4,384,512]{2,1,0:T(8,128)S(1)} %all-to-all-done.y_ref), custom_call_target="tpu_custom_call" | custom-call | flops 7247757312 | bytes 15728640 | tf_op jit(solution)/shard_map/pallas_call | solution.py:212
  121.7 4.2 %fusion.3 = f32[384,256,1]{0,1,2:T(8,128)} fusion(f32[4,384,512]{2,1,0:T(8,128)S(1)} %all-to-all-done.y_ref, f32[4,512,256]{2,1,0:T(8,128)} %bitcast.68), kind=kOutput, calls=%fused_computation.34 | convolution fusion | flops 1207959552 | bytes 5636096 | tf_op jit(solution)/shard_map/gkl,glq->kq/dot_general | solution.py:504
  125.9 4.2 %all-to-all-start.2 = ((f32[4,384,64]{1,2,0:T(8,128)}), f32[4,384,64]{1,2,0:T(8,128)S(1)}, u32[]{:S(2)}, u32[]{:S(2)}) async-start(f32[4,384,64]{1,2,0:T(8,128)} %bitcast.69), calls=%async_computation.2 | async-start | bytes 786432 | tf_op jit(solution)/shard_map/all_to_all | solution.py:506
  130.0 161.7 %shard_map.62 = (f32[256,768]{1,0:T(8,128)}, f32[256,512]{1,0:T(8,128)}, f32[256,1536]{1,0:T(8,128)}) custom-call(f32[4,256,768]{2,1,0:T(8,128)} %copy-done, f32[4,256,512]{2,1,0:T(8,128)} %copy-done.1, f32[4,256,1536]{2,1,0:T(8,128)} %get-tuple-element.27.refs_2_, f32[4,256,512]{2,1,0:T(8,128)} %get-tuple-element.28.refs_3_, ...), custom_call_target="tpu_custom_call" | custom-call | flops 5767168 | bytes 11534336 | tf_op jit(solution)/shard_map/pallas_call | solution.py:433
  291.8 1.1 broadcast_multiply_fusion.2
  292.9 0.1 collective-permute-start.2
  293.0 1.7 broadcast_multiply_fusion
  294.7 0.8 slice.34
  295.5 0.0 collective-permute-start.4
  295.5 0.0 collective-permute-done.2
  295.6 1.1 fusion.2
  296.7 0.0 all-to-all-done.2
  296.7 0.0 copy-done.6
  296.7 4.3 %all-to-all-start.1 = ((f32[4,256,256]{1,2,0:T(8,128)}), f32[4,256,256]{1,2,0:T(8,128)}, u32[]{:S(2)}, u32[]{:S(2)}) async-start(f32[4,256,256]{1,2,0:T(8,128)} %fusion.2), calls=%async_computation.1 | async-start | bytes 2097152 | tf_op jit(solution)/shard_map/all_to_all | solution.py:520
  301.0 0.1 broadcast_multiply_fusion.1
  301.1 10.5 %collective-permute-done.4 = f32[256,512]{1,0:T(8,128)} collective-permute-done((f32[256,512]{1,0:T(8,128)}, f32[256,512]{1,0:T(8,128)}, u32[]{:S(2)}, u32[]{:S(2)}) %collective-permute-start.4) | collective-permute-done | bytes 524320 | tf_op jit(solution)/shard_map/ppermute | solution.py:459
  311.6 0.0 collective-permute-start.5
  311.6 0.8 slice_bitcast_fusion.4
  312.4 0.8 copy.43
  313.2 0.5 copy.34
  313.7 1.1 copy.27
  314.8 0.6 collective-permute-start.3
  315.4 12.4 %collective-permute-done.1 = f32[256,256]{0,1:T(8,128)} collective-permute-done((f32[256,256]{0,1:T(8,128)}, f32[256,256]{0,1:T(8,128)}, u32[]{:S(2)}, u32[]{:S(2)}) %collective-permute-start.1) | collective-permute-done | bytes 262176 | tf_op jit(solution)/shard_map/ppermute | solution.py:459
  327.8 2.2 pad_maximum_fusion.2
  330.0 0.3 copy.39
  330.2 0.2 reshape.86
  330.4 0.9 copy.40
  331.3 2.7 maximum_select_fusion.3
  334.0 0.0 all-to-all-done.1
  334.0 1.6 copy.42
  335.6 0.0 copy-start.4
  335.6 0.1 constant_dynamic-update-slice_fusion
  335.7 1.1 copy-done.4
  336.8 0.1 bitcast_dynamic-update-slice_fusion.6
  336.9 0.1 bitcast_dynamic-update-slice_fusion.4
  337.0 0.1 bitcast_dynamic-update-slice_fusion.2
  337.0 0.1 bitcast_dynamic-update-slice_fusion
  337.1 0.8 copy-done.3
  337.9 0.2 copy-done.7
  338.0 0.1 fusion.1
  338.1 1.6 broadcast_select_fusion
  339.7 0.0 collective-permute-done.3
  339.7 2.4 maximum_select_fusion
  342.2 0.3 slice_bitcast_fusion.2
  342.5 0.9 copy-done.5
  343.4 0.4 pad_maximum_fusion
  343.8 0.2 constant_dynamic-slice_fusion.1
  344.0 0.3 copy.36
  344.4 0.3 copy.37
  344.7 1.5 pad_maximum_fusion.1
  (15 shorter events, 0.1 us)
Async XLA Ops:
  7.2 114.5 %all-gather.3.cloned.1.call-start = ((), (), s32[]{:S(2)}) async-start(), calls=%async_computation.3 | async-start | bytes 2621440 | tf_op jit(solution)/shard_map/all_gather | solution.py:489
  27.9 6.0 %collective-permute-start = (f32[12,128,512]{2,1,0:T(8,128)}, f32[12,128,512]{2,1,0:T(8,128)S(1)}, u32[]{:S(2)}, u32[]{:S(2)}) collective-permute-start(f32[12,128,512]{2,1,0:T(8,128)} %get-tuple-element.19), channel_id=1, source_target_pairs={{0,16},{16,0},{1,17},{17,1},{2,18},{18,2},{3,19},{19,3},{4,20},{20... | collective-permute-start | bytes 9437192 | tf_op jit(solution)/shard_map/ppermute | solution.py:454
  38.2 71.2 %all-to-all-start = ((f32[4,384,512]{2,1,0:T(8,128)}), f32[4,384,512]{2,1,0:T(8,128)S(1)}, u32[]{:S(2)}, u32[]{:S(2)}) async-start(f32[4,384,512]{2,1,0:T(8,128)} %bitcast.59), calls=%async_computation | async-start | bytes 6291456 | tf_op jit(solution)/shard_map/all_to_all | solution.py:492
  77.0 1.6 copy-start
  108.1 1.3 copy-start.1
  125.9 170.8 %all-to-all-start.2 = ((f32[4,384,64]{1,2,0:T(8,128)}), f32[4,384,64]{1,2,0:T(8,128)S(1)}, u32[]{:S(2)}, u32[]{:S(2)}) async-start(f32[4,384,64]{1,2,0:T(8,128)} %bitcast.69), calls=%async_computation.2 | async-start | bytes 786432 | tf_op jit(solution)/shard_map/all_to_all | solution.py:506
  292.9 2.6 copy-start.2
  292.9 2.6 collective-permute-start.2
  295.5 16.1 %collective-permute-start.4 = (f32[256,512]{1,0:T(8,128)}, f32[256,512]{1,0:T(8,128)}, u32[]{:S(2)}, u32[]{:S(2)}) collective-permute-start(f32[256,512]{1,0:T(8,128)} %slice.34), channel_id=1, source_target_pairs={{0,4},{4,8},{8,12},{12,0},{1,5},{5,9},{9,13},{13,1},{2,6},{6,10},{... | collective-permute-start | bytes 1572872 | tf_op jit(solution)/shard_map/ppermute | solution.py:459
  295.5 1.2 copy-start.6
  295.6 5.4 %copy-start.8 = (f32[256,768]{1,0:T(8,128)S(1)}, f32[256,768]{1,0:T(8,128)}, u32[]{:S(2)}) copy-start(f32[256,768]{1,0:T(8,128)} %get-tuple-element.30) | copy-start | bytes 2359300
  296.7 37.3 %all-to-all-start.1 = ((f32[4,256,256]{1,2,0:T(8,128)}), f32[4,256,256]{1,2,0:T(8,128)}, u32[]{:S(2)}, u32[]{:S(2)}) async-start(f32[4,256,256]{1,2,0:T(8,128)} %fusion.2), calls=%async_computation.1 | async-start | bytes 2097152 | tf_op jit(solution)/shard_map/all_to_all | solution.py:520
  311.6 19.7 %collective-permute-start.5 = (f32[512,256]{0,1:T(8,128)}, f32[512,256]{0,1:T(8,128)}, u32[]{:S(2)}, u32[]{:S(2)}) collective-permute-start(f32[512,256]{0,1:T(8,128)} %bitcast.18), channel_id=1, source_target_pairs={{0,16},{16,0},{1,17},{17,1},{2,18},{18,2},{3,19},{19,3},{4,20},{20... | collective-permute-start | bytes 1572872 | tf_op jit(solution)/shard_map/ppermute | solution.py:454
  313.2 14.6 %collective-permute-start.1 = (f32[256,256]{0,1:T(8,128)}, f32[256,256]{0,1:T(8,128)}, u32[]{:S(2)}, u32[]{:S(2)}) collective-permute-start(f32[256,256]{0,1:T(8,128)} %copy.43), channel_id=1, source_target_pairs={{0,4},{4,8},{8,12},{12,0},{1,5},{5,9},{9,13},{13,1},{2,6},{6,10},{... | collective-permute-start | bytes 786440 | tf_op jit(solution)/shard_map/ppermute | solution.py:459
  314.8 24.9 %collective-permute-start.3 = (f32[256,1536]{0,1:T(8,128)S(1)}, f32[256,1536]{0,1:T(8,128)}, u32[]{:S(2)}, u32[]{:S(2)}) collective-permute-start(f32[256,1536]{0,1:T(8,128)S(1)} %copy.34), channel_id=1, source_target_pairs={{0,16},{16,0},{1,17},{17,1},{2,18},{18,2},{3,19},{19,3},{4,20},{20... | collective-permute-start | bytes 4718600 | tf_op jit(solution)/shard_map/ppermute | solution.py:454
  335.6 1.2 copy-start.4
  336.8 1.0 copy-start.3
  336.8 1.2 copy-start.7
  342.1 1.2 copy-start.5
Sparse Core Ops, SparseCore 0:
  28.5 63.7 all-gather.2

commit v3 on v2

--- a/solution.py
+++ b/solution.py
@@ -393,15 +393,16 @@
     for c in range(len(chunks)):
         if chunks[c][0] in given:
             across(c).start()
-    stages, ahead = nbits + 2, 3
+    ahead = min(6, len(chunks))
+    behind = list(range(nbits)) + [nbits + 1, nbits + 3]
     for c in range(ahead):
         first(c)
-    for tick in range(len(chunks) + stages - 1):
+    for tick in range(len(chunks) + behind[-1]):
         if tick + ahead < len(chunks):
             first(tick + ahead)
-        for t in range(stages):
-            if 0 <= tick - t < len(chunks):
-                stage(t, tick - t)
+        for t, late in enumerate(behind):
+            if 0 <= tick - late < len(chunks):
+                stage(t, tick - late)
     for c in range(len(chunks)):
         if chunks[c][0] in given:
             across(c).wait_send()

time: 354 us -> 357 us (level)
  no operation moved by 1% of the time
where the time goes in v3:
time: 357 us; the launch traced here: 356 us
  Pallas kernels  259 us (73%)
  waiting for transfers between devices  26.9 us (8%)
  other arithmetic  19.4 us (5%)
  starting transfers between devices  16.2 us (5%)
  local copies, waits for them, and re-layouts  16 us (4%)
  between operations  14.3 us (4%)
  matrix products  4.18 us (1%)
    pallas_call x1, Pallas kernels, reduce_all(): pl.pallas_call(functools.partial(reduce_kernel, parts, planes, pieces), i...  164 us
    pallas_call x1, Pallas kernels, same_half(): pl.pallas_call(functools.partial(same_half_kernel, parts), grid=(slices,)...  33.7 us
    pallas_call x1, Pallas kernels, cross(): pl.pallas_call(cross_kernel, grid_spec=pltpu.PrefetchScalarGridSpec(num_s...  29.5 us
    ppermute x2, waiting for transfers between devices, mirror(): return lax.ppermute(block, 'gy', perm).T  21.4 us
    pallas_call x1, Pallas kernels, project(): pl.pallas_call(project_kernel, grid=(slices,), in_specs=[pl.BlockSpec((ra...  18.8 us
    pallas_call x1, Pallas kernels, gram_y_terms(): pl.pallas_call(gram_y_kernel, grid_spec=pltpu.PrefetchScalarGridSpec(num_...  12.3 us
    unnamed x25, local copies, waits for them, and re-layouts  9.47 us
  transfers between devices with their start and end apart: 10, of which 3 were waited for; matrix products, arithmetic and copies ran while one was open for 6% of the time, Pallas kernels for 67%

profile of v3, /device:TPU:0, one launch (start us, length us, event | category | flops | bytes accessed | tf_op | source)
XLA Modules:
  0.0 355.6 jit_solution(13984510402039788261)
XLA Ops:
  7.2 0.0 all-gather.3.cloned.1.call-start
  7.2 1.6 copy.25
  8.8 0.3 fusion.u_ref
  9.1 18.8 %shard_map.58 = (f32[12,128,512]{2,1,0:T(8,128)}, f32[12,128,512]{2,1,0:T(8,128)}) custom-call(f32[256,1024]{1,0:T(8,128)S(1)} %fusion.u_ref, f32[12,1024,512]{2,1,0:T(8,128)} %own_ref), custom_call_target="tpu_custom_call" | custom-call | flops 9663676416 | bytes 31457280 | tf_op jit(solution)/shard_map/pallas_call | solution.py:42
  27.9 0.5 collective-permute-start
  28.4 0.0 all-gather.3.cloned.1.call-update
  28.4 5.5 %collective-permute-done = f32[12,128,512]{2,1,0:T(8,128)S(1)} collective-permute-done((f32[12,128,512]{2,1,0:T(8,128)}, f32[12,128,512]{2,1,0:T(8,128)S(1)}, u32[]{:S(2)}, u32[]{:S(2)}) %collective-permute-start) | collective-permute-done | bytes 3145760 | tf_op jit(solution)/shard_map/ppermute | solution.py:455
  33.9 4.3 %add.60 = f32[12,128,512]{2,1,0:T(8,128)} add(f32[12,128,512]{2,1,0:T(8,128)} %get-tuple-element.18, f32[12,128,512]{2,1,0:T(8,128)S(1)} %collective-permute-done) | non-fusion elementwise | flops 786432 | bytes 9437184 | tf_op jit(solution)/shard_map/add | solution.py:487
  38.2 5.1 %all-to-all-start = ((f32[4,384,512]{2,1,0:T(8,128)}), f32[4,384,512]{2,1,0:T(8,128)S(1)}, u32[]{:S(2)}, u32[]{:S(2)}) async-start(f32[4,384,512]{2,1,0:T(8,128)} %bitcast.59), calls=%async_computation | async-start | bytes 6291456 | tf_op jit(solution)/shard_map/all_to_all | solution.py:493
  43.2 33.7 %shard_map.59 = (f32[4,256,768]{2,1,0:T(8,128)S(1)}, f32[6,1024,512]{2,1,0:T(8,128)}) custom-call(f32[12,1024,512]{2,1,0:T(8,128)} %own_ref, f32[12,1024,512]{2,1,0:T(8,128)} %own_ref), custom_call_target="tpu_custom_call" | custom-call | flops 28991029248 | bytes 25165824 | tf_op jit(solution)/shard_map/pallas_call | solution.py:102
  77.0 1.6 copy-done
  78.6 29.5 %shard_map.60 = (f32[4,256,512]{2,1,0:T(8,128)S(1)}, f32[4,256,512]{2,1,0:T(8,128)}) custom-call(s32[1]{0:T(128)} %bitcast.2.gx_ref, f32[12,1024,512]{2,1,0:T(8,128)} %own_ref, f32[6,1024,512]{2,1,0:T(8,128)} %get-tuple-element.24.other_ref), custom_call_target="tpu_custom_call" | custom-call | flops 19327352832 | bytes 25165824 | tf_op jit(solution)/shard_map/pallas_call | solution.py:160
  108.1 1.3 copy-done.1
  109.4 0.0 all-to-all-done.y_ref
  109.4 12.3 %shard_map.61 = (f32[4,256,1536]{2,1,0:T(8,128)}, f32[4,256,1536]{2,1,0:T(8,128)}) custom-call(s32[1]{0:T(128)} %bitcast.2.gx_ref, f32[4,384,512]{2,1,0:T(8,128)S(1)} %all-to-all-done.y_ref), custom_call_target="tpu_custom_call" | custom-call | flops 7247757312 | bytes 15728640 | tf_op jit(solution)/shard_map/pallas_call | solution.py:212
  121.7 4.2 %fusion.3 = f32[384,256,1]{0,1,2:T(8,128)} fusion(f32[4,384,512]{2,1,0:T(8,128)S(1)} %all-to-all-done.y_ref, f32[4,512,256]{2,1,0:T(8,128)} %bitcast.68), kind=kOutput, calls=%fused_computation.34 | convolution fusion | flops 1207959552 | bytes 5636096 | tf_op jit(solution)/shard_map/gkl,glq->kq/dot_general | solution.py:505
  125.9 4.2 %all-to-all-start.2 = ((f32[4,384,64]{1,2,0:T(8,128)}), f32[4,384,64]{1,2,0:T(8,128)S(1)}, u32[]{:S(2)}, u32[]{:S(2)}) async-start(f32[4,384,64]{1,2,0:T(8,128)} %bitcast.69), calls=%async_computation.2 | async-start | bytes 786432 | tf_op jit(solution)/shard_map/all_to_all | solution.py:507
  130.0 164.3 %shard_map.62 = (f32[256,768]{1,0:T(8,128)}, f32[256,512]{1,0:T(8,128)}, f32[256,1536]{1,0:T(8,128)}) custom-call(f32[4,256,768]{2,1,0:T(8,128)} %copy-done, f32[4,256,512]{2,1,0:T(8,128)} %copy-done.1, f32[4,256,1536]{2,1,0:T(8,128)} %get-tuple-element.27.refs_2_, f32[4,256,512]{2,1,0:T(8,128)} %get-tuple-element.28.refs_3_, ...), custom_call_target="tpu_custom_call" | custom-call | flops 5767168 | bytes 11534336 | tf_op jit(solution)/shard_map/pallas_call | solution.py:434
  294.3 1.1 broadcast_multiply_fusion.2
  295.4 0.1 collective-permute-start.2
  295.5 1.7 broadcast_multiply_fusion
  297.2 0.8 slice.34
  298.0 1.4 collective-permute-start.4
  299.5 0.0 collective-permute-done.2
  299.5 1.1 fusion.2
  300.6 0.0 all-to-all-done.2
  300.6 0.0 copy-done.6
  300.6 4.3 %all-to-all-start.1 = ((f32[4,256,256]{1,2,0:T(8,128)}), f32[4,256,256]{1,2,0:T(8,128)}, u32[]{:S(2)}, u32[]{:S(2)}) async-start(f32[4,256,256]{1,2,0:T(8,128)} %fusion.2), calls=%async_computation.1 | async-start | bytes 2097152 | tf_op jit(solution)/shard_map/all_to_all | solution.py:521
  304.9 0.1 broadcast_multiply_fusion.1
  305.0 9.1 %collective-permute-done.4 = f32[256,512]{1,0:T(8,128)} collective-permute-done((f32[256,512]{1,0:T(8,128)}, f32[256,512]{1,0:T(8,128)}, u32[]{:S(2)}, u32[]{:S(2)}) %collective-permute-start.4) | collective-permute-done | bytes 524320 | tf_op jit(solution)/shard_map/ppermute | solution.py:460
  314.1 0.8 slice_bitcast_fusion.4
  314.9 0.8 copy.43
  315.8 0.4 collective-permute-start.1
  316.2 0.5 copy.34
  316.6 1.1 copy.27
  317.7 0.3 collective-permute-start.3
  318.0 12.3 %collective-permute-done.1 = f32[256,256]{0,1:T(8,128)} collective-permute-done((f32[256,256]{0,1:T(8,128)}, f32[256,256]{0,1:T(8,128)}, u32[]{:S(2)}, u32[]{:S(2)}) %collective-permute-start.1) | collective-permute-done | bytes 262176 | tf_op jit(solution)/shard_map/ppermute | solution.py:460
  330.3 2.2 pad_maximum_fusion.2
  332.5 0.3 copy.39
  332.8 0.2 reshape.86
  332.9 0.9 copy.40
  333.8 2.7 maximum_select_fusion.3
  336.6 0.0 all-to-all-done.1
  336.6 1.6 copy.42
  338.1 0.0 copy-start.4
  338.1 0.1 constant_dynamic-update-slice_fusion
  338.2 1.1 copy-done.4
  339.4 0.1 bitcast_dynamic-update-slice_fusion.6
  339.4 0.1 bitcast_dynamic-update-slice_fusion.4
  339.5 0.1 bitcast_dynamic-update-slice_fusion.2
  339.6 0.1 bitcast_dynamic-update-slice_fusion
  339.6 0.8 copy-done.3
  340.4 0.2 copy-done.7
  340.6 0.1 fusion.1
  340.7 1.6 broadcast_select_fusion
  342.2 0.0 collective-permute-done.3
  342.2 2.4 maximum_select_fusion
  344.7 0.3 slice_bitcast_fusion.2
  345.0 0.9 copy-done.5
  345.9 0.4 pad_maximum_fusion
  346.4 0.2 constant_dynamic-slice_fusion.1
  346.6 0.3 copy.36
  346.9 0.3 copy.37
  347.2 1.5 pad_maximum_fusion.1
  (15 shorter events, 0.1 us)
Async XLA Ops:
  7.2 114.5 %all-gather.3.cloned.1.call-start = ((), (), s32[]{:S(2)}) async-start(), calls=%async_computation.3 | async-start | bytes 2621440 | tf_op jit(solution)/shard_map/all_gather | solution.py:490
  27.9 6.0 %collective-permute-start = (f32[12,128,512]{2,1,0:T(8,128)}, f32[12,128,512]{2,1,0:T(8,128)S(1)}, u32[]{:S(2)}, u32[]{:S(2)}) collective-permute-start(f32[12,128,512]{2,1,0:T(8,128)} %get-tuple-element.19), channel_id=1, source_target_pairs={{0,16},{16,0},{1,17},{17,1},{2,18},{18,2},{3,19},{19,3},{4,20},{20... | collective-permute-start | bytes 9437192 | tf_op jit(solution)/shard_map/ppermute | solution.py:455
  38.2 71.2 %all-to-all-start = ((f32[4,384,512]{2,1,0:T(8,128)}), f32[4,384,512]{2,1,0:T(8,128)S(1)}, u32[]{:S(2)}, u32[]{:S(2)}) async-start(f32[4,384,512]{2,1,0:T(8,128)} %bitcast.59), calls=%async_computation | async-start | bytes 6291456 | tf_op jit(solution)/shard_map/all_to_all | solution.py:493
  77.0 1.6 copy-start
  108.1 1.3 copy-start.1
  125.9 174.7 %all-to-all-start.2 = ((f32[4,384,64]{1,2,0:T(8,128)}), f32[4,384,64]{1,2,0:T(8,128)S(1)}, u32[]{:S(2)}, u32[]{:S(2)}) async-start(f32[4,384,64]{1,2,0:T(8,128)} %bitcast.69), calls=%async_computation.2 | async-start | bytes 786432 | tf_op jit(solution)/shard_map/all_to_all | solution.py:507
  295.4 4.0 %copy-start.2 = (f32[256,512]{1,0:T(8,128)}, f32[256,512]{1,0:T(8,128)S(1)}, u32[]{:S(2)}) copy-start(f32[256,512]{1,0:T(8,128)S(1)} %broadcast_multiply_fusion.2) | copy-start | bytes 1572868
  295.4 4.0 %collective-permute-start.2 = (f32[256,512]{1,0:T(8,128)S(1)}, f32[256,512]{1,0:T(8,128)S(1)}, u32[]{:S(2)}, u32[]{:S(2)}) collective-permute-start(f32[256,512]{1,0:T(8,128)S(1)} %broadcast_multiply_fusion.2), channel_id=1, source_target_pairs={{0,16},{16,0},{1,17},{17,1},{2,18},{18,2},{3,19},{19,3},{4,20},{20... | collective-permute-start | bytes 1572872 | tf_op jit(solution)/shard_map/ppermute | solution.py:455
  298.0 16.1 %collective-permute-start.4 = (f32[256,512]{1,0:T(8,128)}, f32[256,512]{1,0:T(8,128)}, u32[]{:S(2)}, u32[]{:S(2)}) collective-permute-start(f32[256,512]{1,0:T(8,128)} %slice.34), channel_id=1, source_target_pairs={{0,4},{4,8},{8,12},{12,0},{1,5},{5,9},{9,13},{13,1},{2,6},{6,10},{... | collective-permute-start | bytes 1572872 | tf_op jit(solution)/shard_map/ppermute | solution.py:460
  299.5 1.2 copy-start.6
  299.5 5.4 %copy-start.8 = (f32[256,768]{1,0:T(8,128)S(1)}, f32[256,768]{1,0:T(8,128)}, u32[]{:S(2)}) copy-start(f32[256,768]{1,0:T(8,128)} %get-tuple-element.30) | copy-start | bytes 2359300
  300.6 35.9 %all-to-all-start.1 = ((f32[4,256,256]{1,2,0:T(8,128)}), f32[4,256,256]{1,2,0:T(8,128)}, u32[]{:S(2)}, u32[]{:S(2)}) async-start(f32[4,256,256]{1,2,0:T(8,128)} %fusion.2), calls=%async_computation.1 | async-start | bytes 2097152 | tf_op jit(solution)/shard_map/all_to_all | solution.py:521
  314.1 19.7 %collective-permute-start.5 = (f32[512,256]{0,1:T(8,128)}, f32[512,256]{0,1:T(8,128)}, u32[]{:S(2)}, u32[]{:S(2)}) collective-permute-start(f32[512,256]{0,1:T(8,128)} %bitcast.18), channel_id=1, source_target_pairs={{0,16},{16,0},{1,17},{17,1},{2,18},{18,2},{3,19},{19,3},{4,20},{20... | collective-permute-start | bytes 1572872 | tf_op jit(solution)/shard_map/ppermute | solution.py:455
  315.8 14.6 %collective-permute-start.1 = (f32[256,256]{0,1:T(8,128)}, f32[256,256]{0,1:T(8,128)}, u32[]{:S(2)}, u32[]{:S(2)}) collective-permute-start(f32[256,256]{0,1:T(8,128)} %copy.43), channel_id=1, source_target_pairs={{0,4},{4,8},{8,12},{12,0},{1,5},{5,9},{9,13},{13,1},{2,6},{6,10},{... | collective-permute-start | bytes 786440 | tf_op jit(solution)/shard_map/ppermute | solution.py:460
  317.7 24.5 %collective-permute-start.3 = (f32[256,1536]{0,1:T(8,128)S(1)}, f32[256,1536]{0,1:T(8,128)}, u32[]{:S(2)}, u32[]{:S(2)}) collective-permute-start(f32[256,1536]{0,1:T(8,128)S(1)} %copy.34), channel_id=1, source_target_pairs={{0,16},{16,0},{1,17},{17,1},{2,18},{18,2},{3,19},{19,3},{4,20},{20... | collective-permute-start | bytes 4718600 | tf_op jit(solution)/shard_map/ppermute | solution.py:455
  338.1 1.2 copy-start.4
  339.4 1.0 copy-start.3
  339.4 1.2 copy-start.7
  344.7 1.2 copy-start.5
Sparse Core Ops, SparseCore 0:
  28.5 63.7 all-gather.2
